TPU v7x, 32 devices: a whole 2x2x4 slice. The times are simulated.
32 devices in a mesh: dp: 4 (over y, x), tensor: 8 (over z, core).
Axes of the slice: x: 2, y: 2, z: 4, core: 2. Of those that a mesh axis runs over, the one named last changes fastest.
Arguments:
- tokens: bfloat16 [8, 1024, 2048], P('dp', 'tensor'), may hold values from -6 to 6
- cotangent: bfloat16 [8, 1024, 2048], P('dp', 'tensor'), may hold values from -6 to 6
- segments: int32 [8, 1024], P('dp'), may hold values from 0 to 5, never falling along the last dimension, each value on 1 to 640 neighbouring positions
- valid_mask: int32 [8, 1024], P('dp'), may hold values 0 or 1
- norm_params: float32 [2, 2048], replicated, may hold values from 0.5 to 1.5
- norm_moments: float32 [2, 2, 2048], replicated, may hold values from 0.0001 to 0.01
- heads_weight: float32 [3, 2048, 2048], P(None, 'dp', 'tensor'), may hold values from -0.125 to 0.125
- heads_moments: float32 [2, 3, 2048, 2048], P(None, None, 'dp', 'tensor'), may hold values from 0.0001 to 0.01
- heads_bias: float32 [3, 2048], P(None, 'tensor'), may hold values from -3 to 3
- heads_bias_moments: float32 [2, 3, 2048], P(None, None, 'tensor'), may hold values from 0.0001 to 0.01
- merge_weight: float32 [2048, 2048], P('tensor', 'dp'), may hold values from -0.5 to 0.5
- merge_moments: float32 [2, 2048, 2048], P(None, 'tensor', 'dp'), may hold values from 0.0001 to 0.01
- expand_weight: float32 [2048, 8192], P('dp', 'tensor'), may hold values from -0.125 to 0.125
- expand_moments: float32 [2, 2048, 8192], P(None, 'dp', 'tensor'), may hold values from 0.0001 to 0.01
- expand_bias: float32 [8192], P('tensor'), may hold values from -3 to 3
- expand_bias_moments: float32 [2, 8192], P(None, 'tensor'), may hold values from 0.0001 to 0.01
- shrink_weight: float32 [8192, 2048], P('tensor', 'dp'), may hold values from -0.0625 to 0.0625
- shrink_moments: float32 [2, 8192, 2048], P(None, 'tensor', 'dp'), may hold values from 0.0001 to 0.01
- output_bias: float32 [2, 2048], replicated, may hold values from -2 to 2
- output_bias_moments: float32 [2, 2, 2048], replicated, may hold values from 0.0001 to 0.01
Outputs:
- output: bfloat16 [8, 1024, 2048], P('dp', 'tensor')
- input_grad: bfloat16 [8, 1024, 2048], P('dp', 'tensor')
- norm_params_update: float32 [2, 2048], replicated
- norm_moments_new: float32 [2, 2, 2048], replicated
- heads_weight_update: float32 [3, 2048, 2048], P(None, 'dp', 'tensor')
- heads_moments_new: float32 [2, 3, 2048, 2048], P(None, None, 'dp', 'tensor')
- heads_bias_update: float32 [3, 2048], P(None, 'tensor')
- heads_bias_moments_new: float32 [2, 3, 2048], P(None, None, 'tensor')
- merge_weight_update: float32 [2048, 2048], P('tensor', 'dp')
- merge_moments_new: float32 [2, 2048, 2048], P(None, 'tensor', 'dp')
- expand_weight_update: float32 [2048, 8192], P('dp', 'tensor')
- expand_moments_new: float32 [2, 2048, 8192], P(None, 'dp', 'tensor')
- expand_bias_update: float32 [8192], P('tensor')
- expand_bias_moments_new: float32 [2, 8192], P(None, 'tensor')
- shrink_weight_update: float32 [8192, 2048], P('tensor', 'dp')
- shrink_moments_new: float32 [2, 8192, 2048], P(None, 'tensor', 'dp')
- output_bias_update: float32 [2, 2048], replicated
- output_bias_moments_new: float32 [2, 2, 2048], replicated
Inputs may be any that keep to these rules, and one draw needn't show every extreme that they name: In each sequence the segments numbers never fall; a document has at most 640 tokens, and one has exactly that many.
All inputs are finite; a program needn't handle non-finite values. No bound on the sum of `valid_mask` on one device may be relied on, other than what follows from the above.
Results may differ from a plain program's by a relative error of at most 0.02.
Values may be sent and summed in bfloat16 or wider, within the bound.
No kernel may reach another device: no remote copies, remote signals or barrier semaphores. Data moves between devices by JAX's collectives and lax.ppermute only.
A program may use at most 256 MiB of HBM per device.

v0:
```python
from functools import partial

import jax
import jax.numpy as jnp
from jax import lax
from jax.sharding import PartitionSpec as P

HEAD_DIM = 64
ROT = 32
STEP = 5


norm_eps = 1e-05
beta_first = 0.9
beta_second = 0.95
adam_eps = 1e-08
masked_score = -1000000000.0


def rotary_tables(segment):
    token_index = jnp.arange(segment.shape[0], dtype=jnp.int32)
    doc_begins = jnp.concatenate([jnp.ones((1,), dtype=jnp.bool_), segment[1:] != segment[:-1]])
    doc_start = lax.cummax(jnp.where(doc_begins, token_index, 0), axis=0)
    positions = (token_index - doc_start).astype(jnp.float32)
    frequency = jnp.power(10000.0, -2.0 * jnp.arange(ROT // 2, dtype=jnp.float32) / ROT)
    angles = positions[:, None] * frequency[None, :]
    return (jnp.cos(angles), jnp.sin(angles))


def rotate(values, cosine_table, sine_table):
    half_rot = ROT // 2
    leading = values[..., :half_rot]
    trailing = values[..., half_rot:ROT]
    cosine_rows = cosine_table[:, None, :]
    sine_rows = sine_table[:, None, :]
    return jnp.concatenate(
        [
            leading * cosine_rows - trailing * sine_rows,
            trailing * cosine_rows + leading * sine_rows,
            values[..., ROT:],
        ],
        axis=-1,
    )


def allowed_mask(segment, valid, start, rows_count):
    query_index = start + jnp.arange(rows_count, dtype=jnp.int32)
    key_index = jnp.arange(segment.shape[0], dtype=jnp.int32)
    query_segment = lax.dynamic_slice_in_dim(segment, start, rows_count, 0)
    same_doc = query_segment[:, None] == segment[None, :]
    causal = key_index[None, :] <= query_index[:, None]
    diagonal = key_index[None, :] == query_index[:, None]
    return same_doc & causal & ((valid[None, :] > 0) | diagonal)


def adam_update(moments, gradient, first_fix, second_fix):
    moment_one = beta_first * moments[0] + (1.0 - beta_first) * gradient
    moment_two = beta_second * moments[1] + (1.0 - beta_second) * gradient * gradient
    scaled_step = moment_one / first_fix / (jnp.sqrt(moment_two / second_fix) + adam_eps)
    return (scaled_step, jnp.stack([moment_one, moment_two]))


def body(
    tokens,
    cotangent,
    segments,
    valid_mask,
    norm_params,
    norm_moments,
    heads_weight,
    heads_moments,
    heads_bias,
    heads_bias_moments,
    merge_weight,
    merge_moments,
    expand_weight,
    expand_moments,
    expand_bias,
    expand_bias_moments,
    shrink_weight,
    shrink_moments,
    output_bias,
    output_bias_moments,
):
    heads_full, merge_full, expand_full, shrink_full = (
        lax.all_gather(heads_weight.astype(jnp.bfloat16), "dp", axis=1, tiled=True),
        lax.all_gather(merge_weight.astype(jnp.bfloat16), "dp", axis=1, tiled=True),
        lax.all_gather(expand_weight.astype(jnp.bfloat16), "dp", axis=0, tiled=True),
        lax.all_gather(shrink_weight.astype(jnp.bfloat16), "dp", axis=1, tiled=True),
    )
    model_width = tokens.shape[2]
    local_width = heads_full.shape[2]
    local_heads = local_width // HEAD_DIM
    seq_len = segments.shape[1]
    norm_gain = norm_params[0]
    norm_shift = norm_params[1]
    score_scale = HEAD_DIM ** (-0.5)
    block_rows = min(512, seq_len)
    block_count = seq_len // block_rows
    block_starts = jnp.arange(block_count, dtype=jnp.int32) * block_rows
    shaped = (seq_len, local_heads, HEAD_DIM)

    def micro_step(carry, seq_entry):
        grads_big, grads_small = carry
        rows_in, cot_rows, segment, valid = seq_entry
        inputs = rows_in.astype(jnp.float32)
        row_mean = jnp.mean(inputs, axis=-1, keepdims=True)
        centred = inputs - row_mean
        variance = jnp.mean(centred * centred, axis=-1, keepdims=True)
        inv_std = lax.rsqrt(variance + norm_eps)
        unit = centred * inv_std
        normed = (unit * norm_gain + norm_shift).astype(jnp.bfloat16)
        normed_full = lax.all_gather(normed, "tensor", axis=0, tiled=True)
        triple = (
            jnp.einsum("sd,tdf->tsf", normed_full, heads_full, preferred_element_type=jnp.float32)
            + heads_bias[:, None, :]
        )
        cosine_table, sine_table = rotary_tables(segment)
        queries = rotate(triple[0].reshape(shaped), cosine_table, sine_table).astype(jnp.bfloat16)
        keys_rot = rotate(triple[1].reshape(shaped), cosine_table, sine_table).astype(jnp.bfloat16)
        values_low = triple[2].reshape(shaped).astype(jnp.bfloat16)
        hidden_pre = (
            jnp.dot(normed_full, expand_full, preferred_element_type=jnp.float32) + expand_bias
        )
        hidden = jax.nn.gelu(hidden_pre, approximate=True).astype(jnp.bfloat16)
        query_blocks = queries.reshape(block_count, block_rows, local_heads, HEAD_DIM)

        def block_scores(query_block, start):
            raw = (
                jnp.einsum(
                    "qhd,khd->hqk", query_block, keys_rot, preferred_element_type=jnp.float32
                )
                * score_scale
            )
            return jnp.where(
                allowed_mask(segment, valid, start, block_rows)[None], raw, masked_score
            )

        def attend(block_item):
            query_block, start = block_item
            scores = block_scores(query_block, start)
            row_max = jnp.max(scores, axis=-1, keepdims=True)
            exponentials = jnp.exp(scores - row_max)
            totals = jnp.sum(exponentials, axis=-1, keepdims=True)
            probs = (exponentials / totals).astype(jnp.bfloat16)
            result = jnp.einsum(
                "hqk,khd->qhd", probs, values_low, preferred_element_type=jnp.float32
            )
            return (result, (row_max + jnp.log(totals))[..., 0])

        attended_blocks, log_totals = lax.map(attend, (query_blocks, block_starts))
        attended = attended_blocks.reshape(seq_len, local_width).astype(jnp.bfloat16)
        attn_sum = lax.psum_scatter(
            jnp.dot(attended, merge_full, preferred_element_type=jnp.float32).astype(jnp.bfloat16),
            "tensor",
            scatter_dimension=0,
            tiled=True,
        ).astype(jnp.float32)
        mlp_sum = lax.psum_scatter(
            jnp.dot(hidden, shrink_full, preferred_element_type=jnp.float32).astype(jnp.bfloat16),
            "tensor",
            scatter_dimension=0,
            tiled=True,
        ).astype(jnp.float32)
        branches = attn_sum + mlp_sum
        output_rows = (inputs + branches + output_bias[0] + output_bias[1]).astype(jnp.bfloat16)
        grad_full = lax.all_gather(cot_rows, "tensor", axis=0, tiled=True)
        d_attended = jnp.einsum(
            "sd,fd->sf", grad_full, merge_full, preferred_element_type=jnp.float32
        ).astype(jnp.bfloat16)
        d_act = jnp.einsum("sd,fd->sf", grad_full, shrink_full, preferred_element_type=jnp.float32)
        merge_step = jnp.einsum(
            "sf,sd->fd", attended, grad_full, preferred_element_type=jnp.float32
        )
        shrink_step = jnp.einsum("sf,sd->fd", hidden, grad_full, preferred_element_type=jnp.float32)
        gelu_pull = jax.vjp(partial(jax.nn.gelu, approximate=True), hidden_pre)[1]
        d_hidden = gelu_pull(d_act)[0].astype(jnp.bfloat16)
        expand_step = jnp.einsum(
            "sd,sf->df", normed_full, d_hidden, preferred_element_type=jnp.float32
        )
        d_out_blocks = d_attended.reshape(block_count, block_rows, local_heads, HEAD_DIM)

        def attend_back(accum, block_item):
            d_keys_acc, d_values_acc = accum
            query_block, start, log_block, d_out_block = block_item
            scores = block_scores(query_block, start)
            probs = jnp.exp(scores - log_block[..., None])
            d_values_acc = d_values_acc + jnp.einsum(
                "hqk,qhd->khd",
                probs.astype(jnp.bfloat16),
                d_out_block,
                preferred_element_type=jnp.float32,
            )
            d_probs = jnp.einsum(
                "qhd,khd->hqk", d_out_block, values_low, preferred_element_type=jnp.float32
            )
            delta = jnp.sum(probs * d_probs, axis=-1, keepdims=True)
            d_scores = (score_scale * probs * (d_probs - delta)).astype(jnp.bfloat16)
            d_query_block = jnp.einsum(
                "hqk,khd->qhd", d_scores, keys_rot, preferred_element_type=jnp.float32
            )
            d_keys_acc = d_keys_acc + jnp.einsum(
                "hqk,qhd->khd", d_scores, query_block, preferred_element_type=jnp.float32
            )
            return ((d_keys_acc, d_values_acc), d_query_block)

        zero_heads = jnp.zeros(shaped, jnp.float32)
        (d_keys_rot, d_values), d_query_blocks = lax.scan(
            attend_back,
            (zero_heads, zero_heads),
            (query_blocks, block_starts, log_totals, d_out_blocks),
        )
        d_queries = rotate(d_query_blocks.reshape(shaped), cosine_table, -sine_table).astype(
            jnp.bfloat16
        )
        d_keys = rotate(d_keys_rot, cosine_table, -sine_table).astype(jnp.bfloat16)
        d_triple = jnp.stack(
            [
                d_queries.reshape(seq_len, local_width),
                d_keys.reshape(seq_len, local_width),
                d_values.reshape(seq_len, local_width).astype(jnp.bfloat16),
            ]
        )
        heads_step = jnp.einsum(
            "sd,tsf->tdf", normed_full, d_triple, preferred_element_type=jnp.float32
        )
        heads_bias_step = jnp.sum(d_triple.astype(jnp.float32), axis=1)
        expand_bias_step = jnp.sum(d_hidden.astype(jnp.float32), axis=0)
        attn_back_sum = lax.psum_scatter(
            jnp.einsum(
                "tsf,tdf->sd", d_triple, heads_full, preferred_element_type=jnp.float32
            ).astype(jnp.bfloat16),
            "tensor",
            scatter_dimension=0,
            tiled=True,
        ).astype(jnp.float32)
        mlp_back_sum = lax.psum_scatter(
            jnp.einsum(
                "sf,df->sd", d_hidden, expand_full, preferred_element_type=jnp.float32
            ).astype(jnp.bfloat16),
            "tensor",
            scatter_dimension=0,
            tiled=True,
        ).astype(jnp.float32)
        d_normed = attn_back_sum + mlp_back_sum
        cot_float = cot_rows.astype(jnp.float32)
        d_unit = d_normed * norm_gain
        mean_unit = jnp.mean(d_unit, axis=-1, keepdims=True)
        mean_cross = jnp.mean(d_unit * unit, axis=-1, keepdims=True)
        grad_rows = (cot_float + inv_std * (d_unit - mean_unit - unit * mean_cross)).astype(
            jnp.bfloat16
        )
        norm_step = jnp.stack([jnp.sum(d_normed * unit, axis=0), jnp.sum(d_normed, axis=0)])
        output_bias_step = jnp.sum(cot_float, axis=0)
        steps_big = (heads_step, merge_step, expand_step, shrink_step)
        grads_big = tuple((summed + fresh for summed, fresh in zip(grads_big, steps_big)))
        steps_small = (norm_step, heads_bias_step, expand_bias_step, output_bias_step)
        grads_small = tuple((summed + fresh for summed, fresh in zip(grads_small, steps_small)))
        return ((grads_big, grads_small), (output_rows, grad_rows))

    big_init = tuple(
        (
            jnp.zeros(weight_copy.shape, jnp.float32)
            for weight_copy in (heads_full, merge_full, expand_full, shrink_full)
        )
    )
    small_init = (
        jnp.zeros((2, model_width), jnp.float32),
        jnp.zeros(heads_bias.shape, jnp.float32),
        jnp.zeros(expand_bias.shape, jnp.float32),
        jnp.zeros((model_width,), jnp.float32),
    )
    (grads_big, grads_small), (output, input_grad) = lax.scan(
        micro_step, (big_init, small_init), (tokens, cotangent, segments, valid_mask)
    )
    grads_big = (
        lax.psum_scatter(
            grads_big[0].astype(jnp.bfloat16), "dp", scatter_dimension=1, tiled=True
        ).astype(jnp.float32),
        lax.psum_scatter(
            grads_big[1].astype(jnp.bfloat16), "dp", scatter_dimension=1, tiled=True
        ).astype(jnp.float32),
        lax.psum_scatter(
            grads_big[2].astype(jnp.bfloat16), "dp", scatter_dimension=0, tiled=True
        ).astype(jnp.float32),
        lax.psum_scatter(
            grads_big[3].astype(jnp.bfloat16), "dp", scatter_dimension=1, tiled=True
        ).astype(jnp.float32),
    )
    heads_bias_total, expand_bias_total = lax.psum((grads_small[1], grads_small[2]), "dp")
    norm_total, output_bias_total = lax.psum((grads_small[0], grads_small[3]), ("dp", "tensor"))
    scale_back = 1.0 / seq_len
    first_fix = 1.0 - beta_first**STEP
    second_fix = 1.0 - beta_second**STEP
    norm_upd, norm_mom = adam_update(norm_moments, norm_total * scale_back, first_fix, second_fix)
    heads_upd, heads_mom = adam_update(
        heads_moments, grads_big[0] * scale_back, first_fix, second_fix
    )
    hbias_upd, hbias_mom = adam_update(
        heads_bias_moments, heads_bias_total * scale_back, first_fix, second_fix
    )
    merge_upd, merge_mom = adam_update(
        merge_moments, grads_big[1] * scale_back, first_fix, second_fix
    )
    expand_upd, expand_mom = adam_update(
        expand_moments, grads_big[2] * scale_back, first_fix, second_fix
    )
    ebias_upd, ebias_mom = adam_update(
        expand_bias_moments, expand_bias_total * scale_back, first_fix, second_fix
    )
    shrink_upd, shrink_mom = adam_update(
        shrink_moments, grads_big[3] * scale_back, first_fix, second_fix
    )
    output_bias_grad = jnp.stack([output_bias_total, output_bias_total]) * scale_back
    obias_upd, obias_mom = adam_update(output_bias_moments, output_bias_grad, first_fix, second_fix)
    return (
        output,
        input_grad,
        norm_upd,
        norm_mom,
        heads_upd,
        heads_mom,
        hbias_upd,
        hbias_mom,
        merge_upd,
        merge_mom,
        expand_upd,
        expand_mom,
        ebias_upd,
        ebias_mom,
        shrink_upd,
        shrink_mom,
        obias_upd,
        obias_mom,
    )


def solution(mesh):
    placed = (
        P("dp", "tensor", None),
        P("dp", "tensor", None),
        P("dp", None),
        P("dp", None),
        P(),
        P(),
        P(None, "dp", "tensor"),
        P(None, None, "dp", "tensor"),
        P(None, "tensor"),
        P(None, None, "tensor"),
        P("tensor", "dp"),
        P(None, "tensor", "dp"),
        P("dp", "tensor"),
        P(None, "dp", "tensor"),
        P("tensor"),
        P(None, "tensor"),
        P("tensor", "dp"),
        P(None, "tensor", "dp"),
        P(),
        P(),
    )
    return jax.shard_map(
        body,
        mesh=mesh,
        in_specs=placed,
        out_specs=(
            P("dp", "tensor", None),
            P("dp", "tensor", None),
            P(),
            P(),
            P(None, "dp", "tensor"),
            P(None, None, "dp", "tensor"),
            P(None, "tensor"),
            P(None, None, "tensor"),
            P("tensor", "dp"),
            P(None, "tensor", "dp"),
            P("dp", "tensor"),
            P(None, "dp", "tensor"),
            P("tensor"),
            P(None, "tensor"),
            P("tensor", "dp"),
            P(None, "tensor", "dp"),
            P(),
            P(),
        ),
        check_vma=False,
    )
```

profile of v0, /device:TPU:0, one launch (start us, length us, event | category | flops | bytes accessed | tf_op | source)
XLA Modules:
  0.0 1184.7 jit_solution(10563647948437791304)
XLA Ops:
  16.4 23.3 %all-gather.13.cloned.1.call-done = bf16[256,2048]{1,0:T(8,128)(2,1)} async-done(((bf16[256,512]{1,0:T(8,128)(2,1)}), bf16[256,2048]{1,0:T(8,128)(2,1)}) %all-gather.13.cloned.1.call-update) | async-done | bytes 1048592 | tf_op jit(solution)/shard_map/all_gather | solution.py:87
  39.7 46.4 %all-gather.11.cloned.1.call-done = bf16[3,2048,256]{2,1,0:T(8,128)(2,1)} async-done(((bf16[3,512,256]{2,1,0:T(8,128)(2,1)}), bf16[3,2048,256]{2,1,0:T(8,128)(2,1)}) %all-gather.11.cloned.1.call-update) | async-done | bytes 3145744 | tf_op jit(solution)/shard_map/all_gather | solution.py:86
  86.1 55.0 %all-gather.15.cloned.1.call-done = bf16[1024,2048]{1,0:T(8,128)(2,1)} async-done(((bf16[1024,512]{1,0:T(8,128)(2,1)}), bf16[1024,2048]{1,0:T(8,128)(2,1)}) %all-gather.15.cloned.1.call-update) | async-done | bytes 4194320 | tf_op jit(solution)/shard_map/all_gather | solution.py:89
  141.1 55.0 %all-gather.17.cloned.1.call-done = bf16[2048,1024]{1,0:T(8,128)(2,1)} async-done(((bf16[512,1024]{1,0:T(8,128)(2,1)}), bf16[2048,1024]{1,0:T(8,128)(2,1)}) %all-gather.17.cloned.1.call-update) | async-done | bytes 4194320 | tf_op jit(solution)/shard_map/all_gather | solution.py:88
  196.1 783.3 %while.92 = (s32[]{:T(128)}, f32[3,2048,256]{1,2,0:T(8,128)}, f32[256,2048]{1,0:T(8,128)}, f32[2048,1024]{1,0:T(8,128)}, f32[1024,2048]{1,0:T(8,128)}, /*index=5...) while((s32[]{:T(128)}, f32[3,2048,256]{1,2,0:T(8,128)}, ...), condition=%wide.region_23.24_spmd.clone.clone, body=%wide.region_0.23_spmd.clone.clone.sunk | while | flops 40693059584 | bytes 724293504 | solution.py:273
  205.0 41.4 %all-gather.19.cloned.1.call-done = bf16[1024,2048]{1,0:T(8,128)(2,1)} async-done(((bf16[128,2048]{1,0:T(8,128)(2,1)}), bf16[1024,2048]{1,0:T(8,128)(2,1)}) %all-gather.19.cloned.1.call-update) | async-done | bytes 4194320 | tf_op jit(solution)/shard_map/while/body/eval_jaxpr/all_gather | solution.py:113
  253.2 24.1 %while.93 = (s32[]{:T(128)}, bf16[2,512,4,64]{1,3,2,0:T(8,128)(2,1)}, f32[2,4,512]{2,1,0:T(4,128)S(1)}, s32[2]{0:T(128)S(1)}, s32[1024]{0:T(1024)S(1)}, /*index=...) while((s32[]{:T(128)}, ...), condition=%wide.region_8.8_spmd, body=%wide.region_5.7_spmd.sunk | while | flops 565181952 | bytes 33378544 | solution.py:151
  277.3 16.5 %all-gather.21.cloned.1.call-done = bf16[1,1024,2048]{2,1,0:T(8,128)(2,1)} async-done(((bf16[1,128,2048]{2,1,0:T(8,128)(2,1)}), bf16[1,1024,2048]{2,1,0:T(8,128)(2,1)}) %all-gather.21.cloned.1.call-update) | async-done | bytes 4194320 | tf_op jit(solution)/shard_map/while/body/eval_jaxpr/all_gather | solution.py:167
  301.3 69.8 %while.94 = (s32[]{:T(128)}, f32[1024,4,64]{0,2,1:T(8,128)S(1)}, f32[1024,4,64]{0,2,1:T(8,128)}, f32[2,512,4,64]{1,0,3,2:T(2,128)}, bf16[2,512,4,64]{1,3,2,0:T(8...) while((s32[]{:T(128)}, f32[1024,4,64]{0,2,1:T(8,128)S(1)}, ...), condition=%wide.region_11.11_spmd.clone, body=%wide.region_9.10_spmd.clone.sunk | while | flops 1379925504 | bytes 166801840 | solution.py:208
  317.3 10.4 dynamic_update_slice.40
  351.3 10.4 dynamic_update_slice.40
  380.9 7.7 fusion.239
  408.4 10.5 convolution_convert_fusion.7
  448.2 32.9 %reduce-scatter.17.cloned.1.call-done = bf16[128,2048]{1,0:T(8,128)(2,1)} async-done(((bf16[1024,2048]{1,0:T(8,128)(2,1)}), bf16[128,2048]{1,0:T(8,128)(2,1)}) %reduce-scatter.17.cloned.1.call-update) | async-done | bytes 524304 | tf_op jit(solution)/shard_map/while/body/eval_jaxpr/reduce_scatter | solution.py:237
  483.0 48.8 %reduce-scatter.23.cloned.1.call-done = bf16[128,2048]{1,0:T(8,128)(2,1)} async-done(((bf16[1024,2048]{1,0:T(8,128)(2,1)}), bf16[128,2048]{1,0:T(8,128)(2,1)}) %reduce-scatter.23.cloned.1.call-update) | async-done | bytes 524304 | tf_op jit(solution)/shard_map/while/body/eval_jaxpr/reduce_scatter | solution.py:153
  531.7 50.4 %reduce-scatter.21.cloned.1.call-done = bf16[128,2048]{1,0:T(8,128)(2,1)} async-done(((bf16[1024,2048]{1,0:T(8,128)(2,1)}), bf16[128,2048]{1,0:T(8,128)(2,1)}) %reduce-scatter.21.cloned.1.call-update) | async-done | bytes 524304 | tf_op jit(solution)/shard_map/while/body/eval_jaxpr/reduce_scatter | solution.py:159
  594.6 39.5 %all-gather.19.cloned.1.call-done = bf16[1024,2048]{1,0:T(8,128)(2,1)} async-done(((bf16[128,2048]{1,0:T(8,128)(2,1)}), bf16[1024,2048]{1,0:T(8,128)(2,1)}) %all-gather.19.cloned.1.call-update) | async-done | bytes 4194320 | tf_op jit(solution)/shard_map/while/body/eval_jaxpr/all_gather | solution.py:113
  641.0 24.1 %while.93 = (s32[]{:T(128)}, bf16[2,512,4,64]{1,3,2,0:T(8,128)(2,1)}, f32[2,4,512]{2,1,0:T(4,128)S(1)}, s32[2]{0:T(128)S(1)}, s32[1024]{0:T(1024)S(1)}, /*index=...) while((s32[]{:T(128)}, ...), condition=%wide.region_8.8_spmd, body=%wide.region_5.7_spmd.sunk | while | flops 565181952 | bytes 33378544 | solution.py:151
  665.1 16.5 %all-gather.21.cloned.1.call-done = bf16[1,1024,2048]{2,1,0:T(8,128)(2,1)} async-done(((bf16[1,128,2048]{2,1,0:T(8,128)(2,1)}), bf16[1,1024,2048]{2,1,0:T(8,128)(2,1)}) %all-gather.21.cloned.1.call-update) | async-done | bytes 4194320 | tf_op jit(solution)/shard_map/while/body/eval_jaxpr/all_gather | solution.py:167
  689.1 69.6 %while.94 = (s32[]{:T(128)}, f32[1024,4,64]{0,2,1:T(8,128)S(1)}, f32[1024,4,64]{0,2,1:T(8,128)}, f32[2,512,4,64]{1,0,3,2:T(2,128)}, bf16[2,512,4,64]{1,3,2,0:T(8...) while((s32[]{:T(128)}, f32[1024,4,64]{0,2,1:T(8,128)S(1)}, ...), condition=%wide.region_11.11_spmd.clone, body=%wide.region_9.10_spmd.clone.sunk | while | flops 1379925504 | bytes 166801840 | solution.py:208
  704.9 10.4 dynamic_update_slice.40
  739.0 10.4 dynamic_update_slice.40
  796.0 10.5 convolution_convert_fusion.7
  813.2 8.7 bitcast_add_fusion.6
  831.3 9.8 select_add_fusion.11
  841.1 27.4 %reduce-scatter.17.cloned.1.call-done = bf16[128,2048]{1,0:T(8,128)(2,1)} async-done(((bf16[1024,2048]{1,0:T(8,128)(2,1)}), bf16[128,2048]{1,0:T(8,128)(2,1)}) %reduce-scatter.17.cloned.1.call-update) | async-done | bytes 524304 | tf_op jit(solution)/shard_map/while/body/eval_jaxpr/reduce_scatter | solution.py:237
  870.4 48.6 %reduce-scatter.23.cloned.1.call-done = bf16[128,2048]{1,0:T(8,128)(2,1)} async-done(((bf16[1024,2048]{1,0:T(8,128)(2,1)}), bf16[128,2048]{1,0:T(8,128)(2,1)}) %reduce-scatter.23.cloned.1.call-update) | async-done | bytes 524304 | tf_op jit(solution)/shard_map/while/body/eval_jaxpr/reduce_scatter | solution.py:153
  918.9 50.4 %reduce-scatter.21.cloned.1.call-done = bf16[128,2048]{1,0:T(8,128)(2,1)} async-done(((bf16[1024,2048]{1,0:T(8,128)(2,1)}), bf16[128,2048]{1,0:T(8,128)(2,1)}) %reduce-scatter.21.cloned.1.call-update) | async-done | bytes 524304 | tf_op jit(solution)/shard_map/while/body/eval_jaxpr/reduce_scatter | solution.py:159
  1000.7 10.5 all-reduce.1
  1012.4 37.2 %all-reduce = (f32[2,2048]{1,0:T(2,128)S(1)}, f32[2048]{0:T(1024)S(1)}) all-reduce(f32[2,2048]{1,0:T(2,128)S(1)} %copy-done.32, f32[2048]{0:T(1024)S(1)} %copy-done.36), channel_id=1, replica_groups=mesh['dp'=4,'tensor'=8] {'dp','tensor'}, use_global_device_ids=true, to_apply=%region_24.25 | all-reduce | flops 6144 | bytes 49152 | tf_op jit(solution)/shard_map/psum | solution.py:291
  1063.8 50.1 %reduce-scatter.15.cloned.1.call-done = bf16[1024,512]{1,0:T(8,128)(2,1)} async-done(((bf16[1024,2048]{1,0:T(8,128)(2,1)}), bf16[1024,512]{1,0:T(8,128)(2,1)}) %reduce-scatter.15.cloned.1.call-update) | async-done | bytes 1048592 | tf_op jit(solution)/shard_map/reduce_scatter | solution.py:286
  1121.6 48.4 %reduce-scatter.13.cloned.1.call-done = bf16[512,1024]{1,0:T(8,128)(2,1)} async-done(((bf16[2048,1024]{1,0:T(8,128)(2,1)}), bf16[512,1024]{1,0:T(8,128)(2,1)}) %reduce-scatter.13.cloned.1.call-update) | async-done | bytes 1048592 | tf_op jit(solution)/shard_map/reduce_scatter | solution.py:283
  (565 shorter events, 357.4 us)
Async XLA Ops:
  7.2 32.5 %all-gather.13.cloned.1.call-start = ((), (), s32[]{:S(2)}) async-start(), calls=%async_computation.9 | async-start | bytes 1310720 | tf_op jit(solution)/shard_map/all_gather | solution.py:87
  9.2 76.9 %all-gather.11.cloned.1.call-start = ((), (), s32[]{:S(2)}) async-start(), calls=%async_computation.8 | async-start | bytes 3932160 | tf_op jit(solution)/shard_map/all_gather | solution.py:86
  11.6 184.5 %copy-start.5 = (bf16[2,128,2048]{2,1,0:T(8,128)(2,1)S(1)}, bf16[2,128,2048]{2,1,0:T(8,128)(2,1)}, u32[]{:S(2)}) copy-start(bf16[2,128,2048]{2,1,0:T(8,128)(2,1)} %param.26) | copy-start | bytes 3145732
  11.7 184.5 %copy-start.56 = (f32[3,256]{1,0:T(4,128)S(1)}, f32[3,256]{1,0:T(4,128)}, u32[]{:S(2)}) copy-start(f32[3,256]{1,0:T(4,128)} %param.34) | copy-start | bytes 9220
  11.7 129.4 %all-gather.15.cloned.1.call-start = ((), (), s32[]{:S(2)}) async-start(), calls=%async_computation.10 | async-start | bytes 5242880 | tf_op jit(solution)/shard_map/all_gather | solution.py:89
  12.9 183.3 %all-gather.17.cloned.1.call-start = ((), (), s32[]{:S(2)}) async-start(), calls=%async_computation.11 | async-start | bytes 5242880 | tf_op jit(solution)/shard_map/all_gather | solution.py:88
  196.1 50.3 %all-gather.19.cloned.1.call-start = ((), (), s32[]{:S(2)}) async-start(), calls=%async_computation.16 | async-start | bytes 4718592 | tf_op jit(solution)/shard_map/while/body/eval_jaxpr/all_gather | solution.py:113
  199.1 94.7 %all-gather.21.cloned.1.call-start = ((), (), s32[]{:S(2)}) async-start(), calls=%async_computation.17 | async-start | bytes 4718592 | tf_op jit(solution)/shard_map/while/body/eval_jaxpr/all_gather | solution.py:167
  201.7 246.6 %reduce-scatter.19.cloned.1.call-start = ((), (), s32[]{:S(2)}) async-start(), calls=%async_computation.19 | async-start | bytes 4718592 | tf_op jit(solution)/shard_map/while/body/eval_jaxpr/reduce_scatter | solution.py:229
  301.3 72.1 %copy-start.21 = (f32[1024,16]{0,1:T(8,128)S(1)}, f32[1024,16]{0,1:T(8,128)}, u32[]{:S(2)}) copy-start(f32[1024,16]{0,1:T(8,128)} %copy-done.20) | copy-start | bytes 196612 | tf_op jit(solution)/shard_map/while
  301.3 72.1 %copy-start.26 = (f32[1024,16]{0,1:T(8,128)S(1)}, f32[1024,16]{0,1:T(8,128)}, u32[]{:S(2)}) copy-start(f32[1024,16]{0,1:T(8,128)} %get-tuple-element.1186) | copy-start | bytes 196612 | tf_op jit(solution)/shard_map/while
  380.8 100.3 %reduce-scatter.17.cloned.1.call-start = ((), (), s32[]{:S(2)}) async-start(), calls=%async_computation.18 | async-start | bytes 4718592 | tf_op jit(solution)/shard_map/while/body/eval_jaxpr/reduce_scatter | solution.py:237
  403.4 128.3 %reduce-scatter.23.cloned.1.call-start = ((), (), s32[]{:S(2)}) async-start(), calls=%async_computation.21 | async-start | bytes 4718592 | tf_op jit(solution)/shard_map/while/body/eval_jaxpr/reduce_scatter | solution.py:153
  408.4 173.8 %reduce-scatter.21.cloned.1.call-start = ((), (), s32[]{:S(2)}) async-start(), calls=%async_computation.20 | async-start | bytes 4718592 | tf_op jit(solution)/shard_map/while/body/eval_jaxpr/reduce_scatter | solution.py:159
  440.8 141.3 %copy-start.9 = (bf16[1,128,2048]{2,1,0:T(8,128)(2,1)S(1)}, bf16[1,128,2048]{2,1,0:T(8,128)(2,1)}, u32[]{:S(2)}) copy-start(bf16[1,128,2048]{2,1,0:T(8,128)(2,1)} %get-tuple-element.1182) | copy-start | bytes 1572868 | tf_op jit(solution)/shard_map/while
  448.2 137.3 %copy-start.57 = (f32[3,256]{1,0:T(4,128)S(1)}, f32[3,256]{1,0:T(4,128)}, u32[]{:S(2)}) copy-start(f32[3,256]{1,0:T(4,128)} %get-tuple-element.1547) | copy-start | bytes 9220 | tf_op jit(solution)/shard_map/while
  483.0 102.6 %copy-start.31 = (f32[2,2048]{1,0:T(2,128)}, f32[2,2048]{1,0:T(2,128)S(1)}, u32[]{:S(2)}) copy-start(f32[2,2048]{1,0:T(2,128)S(1)} %maximum_add_fusion.2) | copy-start | bytes 49156 | tf_op jit(solution)/shard_map/while
  585.7 48.5 %all-gather.19.cloned.1.call-start = ((), (), s32[]{:S(2)}) async-start(), calls=%async_computation.16 | async-start | bytes 4718592 | tf_op jit(solution)/shard_map/while/body/eval_jaxpr/all_gather | solution.py:113
  588.7 92.9 %all-gather.21.cloned.1.call-start = ((), (), s32[]{:S(2)}) async-start(), calls=%async_computation.17 | async-start | bytes 4718592 | tf_op jit(solution)/shard_map/while/body/eval_jaxpr/all_gather | solution.py:167
  591.3 249.8 %reduce-scatter.19.cloned.1.call-start = ((), (), s32[]{:S(2)}) async-start(), calls=%async_computation.19 | async-start | bytes 4718592 | tf_op jit(solution)/shard_map/while/body/eval_jaxpr/reduce_scatter | solution.py:229
  689.1 71.9 %copy-start.21 = (f32[1024,16]{0,1:T(8,128)S(1)}, f32[1024,16]{0,1:T(8,128)}, u32[]{:S(2)}) copy-start(f32[1024,16]{0,1:T(8,128)} %copy-done.20) | copy-start | bytes 196612 | tf_op jit(solution)/shard_map/while
  689.1 71.9 %copy-start.26 = (f32[1024,16]{0,1:T(8,128)S(1)}, f32[1024,16]{0,1:T(8,128)}, u32[]{:S(2)}) copy-start(f32[1024,16]{0,1:T(8,128)} %get-tuple-element.1186) | copy-start | bytes 196612 | tf_op jit(solution)/shard_map/while
  768.5 100.0 %reduce-scatter.17.cloned.1.call-start = ((), (), s32[]{:S(2)}) async-start(), calls=%async_computation.18 | async-start | bytes 4718592 | tf_op jit(solution)/shard_map/while/body/eval_jaxpr/reduce_scatter | solution.py:237
  791.0 127.9 %reduce-scatter.23.cloned.1.call-start = ((), (), s32[]{:S(2)}) async-start(), calls=%async_computation.21 | async-start | bytes 4718592 | tf_op jit(solution)/shard_map/while/body/eval_jaxpr/reduce_scatter | solution.py:153
  796.0 173.4 %reduce-scatter.21.cloned.1.call-start = ((), (), s32[]{:S(2)}) async-start(), calls=%async_computation.20 | async-start | bytes 4718592 | tf_op jit(solution)/shard_map/while/body/eval_jaxpr/reduce_scatter | solution.py:159
  831.3 138.1 %copy-start.9 = (bf16[1,128,2048]{2,1,0:T(8,128)(2,1)S(1)}, bf16[1,128,2048]{2,1,0:T(8,128)(2,1)}, u32[]{:S(2)}) copy-start(bf16[1,128,2048]{2,1,0:T(8,128)(2,1)} %get-tuple-element.1182) | copy-start | bytes 1572868 | tf_op jit(solution)/shard_map/while
  841.1 131.7 %copy-start.57 = (f32[3,256]{1,0:T(4,128)S(1)}, f32[3,256]{1,0:T(4,128)}, u32[]{:S(2)}) copy-start(f32[3,256]{1,0:T(4,128)} %get-tuple-element.1547) | copy-start | bytes 9220 | tf_op jit(solution)/shard_map/while
  870.3 102.4 %copy-start.31 = (f32[2,2048]{1,0:T(2,128)}, f32[2,2048]{1,0:T(2,128)S(1)}, u32[]{:S(2)}) copy-start(f32[2,2048]{1,0:T(2,128)S(1)} %maximum_add_fusion.2) | copy-start | bytes 49156 | tf_op jit(solution)/shard_map/while
  979.4 73.5 %reduce-scatter.11.cloned.1.call-start = ((), (), s32[]{:S(2)}) async-start(), calls=%async_computation.13 | async-start | bytes 1310720 | tf_op jit(solution)/shard_map/reduce_scatter | solution.py:280
  982.2 75.4 %reduce-scatter.9.cloned.1.call-start = ((), (), s32[]{:S(2)}) async-start(), calls=%async_computation.12 | async-start | bytes 3932160 | tf_op jit(solution)/shard_map/reduce_scatter | solution.py:277
  987.6 126.3 %reduce-scatter.15.cloned.1.call-start = ((), (), s32[]{:S(2)}) async-start(), calls=%async_computation.15 | async-start | bytes 5242880 | tf_op jit(solution)/shard_map/reduce_scatter | solution.py:286
  993.8 176.2 %reduce-scatter.13.cloned.1.call-start = ((), (), s32[]{:S(2)}) async-start(), calls=%async_computation.14 | async-start | bytes 5242880 | tf_op jit(solution)/shard_map/reduce_scatter | solution.py:283
  (123 other events, 1014.2 us)
Sparse Core Ops, SparseCore 0:
  10.4 29.1 all-gather.12
  42.1 43.9 all-gather.10
  88.5 52.5 all-gather.14
  143.4 52.6 all-gather.16
  199.2 47.1 all-gather.18
  247.9 45.8 all-gather.20
  381.0 48.9 reduce-scatter.18
  433.0 48.1 reduce-scatter.16
  483.5 48.1 reduce-scatter.22
  534.0 48.1 reduce-scatter.20
  588.8 45.3 all-gather.18
  635.7 45.8 all-gather.20
  768.6 48.8 reduce-scatter.18
  820.3 48.1 reduce-scatter.16
  870.8 48.1 reduce-scatter.22
  921.2 48.1 reduce-scatter.20
  983.4 26.0 reduce-scatter.10
  1013.2 44.3 reduce-scatter.8
  1061.4 52.4 reduce-scatter.14
  1117.3 52.6 reduce-scatter.12
where the time goes:
time: 1190 us; the launch traced here: 1180 us
  waiting for transfers between devices  653 us (55%)
  matrix products  224 us (19%)
  other arithmetic  113 us (9%)
  local copies, waits for them, and re-layouts  107 us (9%)
  blocking collectives  47.7 us (4%)
  loops' own time  25.6 us (2%)
  between operations  14.6 us (1%)
    reduce_scatter x2, waiting for transfers between devices, micro_step(): lax.psum_scatter(jnp.dot(hidden, shrink_full, preferred_element_type=jnp....  101 us
    reduce_scatter x2, waiting for transfers between devices, micro_step(): lax.psum_scatter(jnp.dot(attended, merge_full, preferred_element_type=jnp...  97.3 us
    all_gather x2, waiting for transfers between devices, micro_step(): normed_full = lax.all_gather(normed, 'tensor', axis=0, tiled=True)  80.9 us
    reduce_scatter x2, waiting for transfers between devices, micro_step(): lax.psum_scatter(jnp.einsum('sf,df->sd', d_hidden, expand_full, preferred...  60.3 us
    all_gather x1, waiting for transfers between devices, body(): lax.all_gather(expand_weight.astype(jnp.bfloat16), 'dp', axis=0, tiled=True)  55 us
    all_gather x1, waiting for transfers between devices, body(): lax.all_gather(shrink_weight.astype(jnp.bfloat16), 'dp', axis=1, tiled=True)  55 us
    reduce_scatter x1, waiting for transfers between devices, body(): lax.psum_scatter(grads_big[3].astype(jnp.bfloat16), 'dp', scatter_dimensi...  50.1 us
    reduce_scatter x1, waiting for transfers between devices, body(): lax.psum_scatter(grads_big[2].astype(jnp.bfloat16), 'dp', scatter_dimensi...  48.4 us
  transfers between devices with their start and end apart: 20, of which 17 were waited for; matrix products, arithmetic and copies ran while one was open for 20% of the time, Pallas kernels for 0%

commit v1 on v0

v1 whole, which is shorter than its diff:
```python
import jax
import jax.numpy as jnp
from jax import lax
from jax.experimental import pallas as pl
from jax.experimental.pallas import tpu as pltpu
from jax.sharding import PartitionSpec as P

HEAD_DIM = 64
ROT = 32
STEP = 5
LANES = 128

norm_eps = 1e-05
beta_first = 0.9
beta_second = 0.95
adam_eps = 1e-08
masked_score = -1000000000.0
score_scale = HEAD_DIM ** (-0.5)

f32 = jnp.float32
bf16 = jnp.bfloat16


def document_starts(segment):
    token_index = jnp.arange(segment.shape[0], dtype=jnp.int32)
    doc_begins = jnp.concatenate([jnp.ones((1,), dtype=jnp.bool_), segment[1:] != segment[:-1]])
    return lax.cummax(jnp.where(doc_begins, token_index, 0), axis=0)


def rotary_tables(doc_start):
    seq_len = doc_start.shape[0]
    positions = (jnp.arange(seq_len, dtype=jnp.int32) - doc_start).astype(f32)
    frequency = jnp.power(10000.0, -2.0 * jnp.arange(ROT // 2, dtype=f32) / ROT)
    angles = positions[:, None] * frequency[None, :]
    cosine, sine = jnp.cos(angles), jnp.sin(angles)
    rest = HEAD_DIM - ROT
    cosine = jnp.concatenate([cosine, cosine, jnp.ones((seq_len, rest), f32)], axis=1)
    sine = jnp.concatenate([-sine, sine, jnp.zeros((seq_len, rest), f32)], axis=1)
    copies = LANES // HEAD_DIM
    return jnp.tile(cosine, (1, copies)), jnp.tile(sine, (1, copies))


def masks(doc_start, valid):
    index = jnp.arange(doc_start.shape[0], dtype=jnp.int32)

    def build(query, start, key, key_valid):
        allowed = (key >= start) & (key <= query) & ((key_valid > 0) | (key == query))
        return jnp.where(allowed, 0.0, masked_score).astype(bf16)

    rows = build(index[:, None], doc_start[:, None], index[None, :], valid[None, :])
    columns = build(index[None, :], doc_start[None, :], index[:, None], valid[:, None])
    return rows, columns


def rotate(values, cosine, sine):
    half_rot = ROT // 2
    width = values.shape[1]
    lane = lax.broadcasted_iota(jnp.int32, values.shape, 1) % HEAD_DIM
    ahead = pltpu.roll(values, width - half_rot, 1)
    behind = pltpu.roll(values, half_rot, 1)
    partner = jnp.where(lane < half_rot, ahead, behind)
    return values * cosine + partner * sine


def nt(left, right):
    return lax.dot_general(left, right, (((1,), (1,)), ((), ())), preferred_element_type=f32)


def nn(left, right):
    return lax.dot_general(left, right, (((1,), (0,)), ((), ())), preferred_element_type=f32)


def tn(left, right):
    return lax.dot_general(left, right, (((0,), (0,)), ((), ())), preferred_element_type=f32)


def widen(table, width):
    return jnp.concatenate([table] * (width // LANES), axis=1)


def attend_kernel(
    low_ref, triple_ref, bias_ref, cos_ref, sin_ref, mask_ref, qkv_ref, out_ref, lse_ref, k_all, v_all
):
    step = pl.program_id(0)
    rows, width = out_ref.shape
    heads = width // HEAD_DIM
    blocks = k_all.shape[0] // rows
    cosine = widen(cos_ref[...], width)
    sine = widen(sin_ref[...], width)
    query = rotate(triple_ref[:, :width] + bias_ref[0:1, :], cosine, sine).astype(bf16)
    key = rotate(triple_ref[:, width : 2 * width] + bias_ref[1:2, :], cosine, sine).astype(bf16)
    value = (triple_ref[:, 2 * width :] + bias_ref[2:3, :]).astype(bf16)
    qkv_ref[0] = query
    qkv_ref[1] = key
    qkv_ref[2] = value
    own = pl.ds(pl.multiple_of(step * rows, rows), rows)
    k_all[own, :] = key
    v_all[own, :] = value
    scaled = query * jnp.asarray(score_scale, bf16)
    head_of = lax.broadcasted_iota(jnp.int32, (rows, width), 1) // HEAD_DIM
    lane = lax.broadcasted_iota(jnp.int32, (rows, LANES), 1)
    span = step - low_ref[step] + 1
    for count in range(1, blocks + 1):

        @pl.when(span == count)
        def _(count=count):
            begin = pl.multiple_of((step - (count - 1)) * rows, rows)
            keys = k_all[pl.ds(begin, count * rows), :]
            values = v_all[pl.ds(begin, count * rows), :]
            mask = mask_ref[:, pl.ds(begin, count * rows)].astype(f32)
            result = jnp.zeros((rows, width), f32)
            stats = jnp.zeros((rows, LANES), f32)
            for head in range(heads):
                mine = head_of == head
                scores = nt(jnp.where(mine, scaled, jnp.zeros_like(scaled)), keys) + mask
                top = jnp.max(scores, axis=1, keepdims=True)
                weights = jnp.exp(scores - top)
                total = jnp.sum(weights, axis=1, keepdims=True)
                mixed = nn(weights.astype(bf16), values) * (1.0 / total)
                result = jnp.where(mine, mixed, result)
                stats = jnp.where(lane == head, top + jnp.log(total), stats)
            out_ref[...] = result.astype(bf16)
            lse_ref[...] = jnp.transpose(stats)[: lse_ref.shape[0], :]


def attend(triple, bias, cosine, sine, mask, low, rows):
    seq_len = triple.shape[0]
    width = triple.shape[1] // 3
    blocks = seq_len // rows
    stat_rows = 8
    grid_spec = pltpu.PrefetchScalarGridSpec(
        num_scalar_prefetch=1,
        grid=(blocks,),
        in_specs=[
            pl.BlockSpec((rows, 3 * width), lambda i, low: (i, 0)),
            pl.BlockSpec((3, width), lambda i, low: (0, 0)),
            pl.BlockSpec((rows, LANES), lambda i, low: (i, 0)),
            pl.BlockSpec((rows, LANES), lambda i, low: (i, 0)),
            pl.BlockSpec((rows, seq_len), lambda i, low: (i, 0)),
        ],
        out_specs=[
            pl.BlockSpec((3, rows, width), lambda i, low: (0, i, 0)),
            pl.BlockSpec((rows, width), lambda i, low: (i, 0)),
            pl.BlockSpec((stat_rows, rows), lambda i, low: (0, i)),
        ],
        scratch_shapes=[pltpu.VMEM((seq_len, width), bf16), pltpu.VMEM((seq_len, width), bf16)],
    )
    pairs = seq_len * seq_len * width
    return pl.pallas_call(
        attend_kernel,
        grid_spec=grid_spec,
        out_shape=[
            jax.ShapeDtypeStruct((3, seq_len, width), bf16),
            jax.ShapeDtypeStruct((seq_len, width), bf16),
            jax.ShapeDtypeStruct((stat_rows, seq_len), f32),
        ],
        compiler_params=pltpu.CompilerParams(vmem_limit_bytes=24 * 1024 * 1024),
        cost_estimate=pl.CostEstimate(
            flops=4 * pairs, bytes_accessed=8 * seq_len * seq_len, transcendentals=pairs // HEAD_DIM
        ),
        name="attend",
    )(low, triple, bias, cosine, sine, mask)


def attend_back_kernel(
    low_ref, q_ref, k_ref, v_ref, d_ref, lse_ref, mask_ref, cos_ref, sin_ref, out_ref, sum_ref, dk_all, dv_all
):
    step = pl.program_id(0)
    rows, width = d_ref.shape
    heads = width // HEAD_DIM
    seq_len = dk_all.shape[0]
    blocks = seq_len // rows

    @pl.when(step == 0)
    def _():
        dk_all[...] = jnp.zeros_like(dk_all)
        dv_all[...] = jnp.zeros_like(dv_all)
        sum_ref[...] = jnp.zeros_like(sum_ref)

    scaled = q_ref[0] * jnp.asarray(score_scale, bf16)
    d_out = d_ref[...]
    zero = jnp.zeros_like(d_out)
    head_of = lax.broadcasted_iota(jnp.int32, (rows, width), 1) // HEAD_DIM
    own = pl.ds(pl.multiple_of(step * rows, rows), rows)
    span = step - low_ref[step] + 1
    for count in range(1, blocks + 1):

        @pl.when(span == count)
        def _(count=count):
            begin = pl.multiple_of((step - (count - 1)) * rows, rows)
            reach = pl.ds(begin, count * rows)
            keys = k_ref[0, reach, :]
            values = v_ref[0, reach, :]
            mask = mask_ref[reach, :].astype(f32)
            d_query = jnp.zeros((rows, width), f32)
            probs_side, scores_side, queries_down, d_outs_down = [], [], [], []
            for head in range(heads):
                mine = head_of == head
                query = jnp.where(mine, scaled, zero)
                d_mine = jnp.where(mine, d_out, zero)
                scores = nt(keys, query) + mask
                probs = jnp.exp(scores - lse_ref[head : head + 1, :])
                d_probs = nt(values, d_mine)
                delta = jnp.sum(probs * d_probs, axis=0, keepdims=True)
                d_scores = (probs * (d_probs - delta)).astype(bf16)
                d_query = jnp.where(mine, tn(d_scores, keys), d_query)
                probs_side.append(probs.astype(bf16))
                scores_side.append(d_scores)
                queries_down.append(query)
                d_outs_down.append(d_mine)
            dv_all[reach, :] += nn(
                jnp.concatenate(probs_side, axis=1), jnp.concatenate(d_outs_down, axis=0)
            )
            dk_all[reach, :] += nn(
                jnp.concatenate(scores_side, axis=1), jnp.concatenate(queries_down, axis=0)
            )
            cosine = widen(cos_ref[own, :], width)
            sine = widen(sin_ref[own, :], width)
            low_query = rotate(d_query * score_scale, cosine, -sine).astype(bf16)
            out_ref[own, :width] = low_query
            sum_ref[0:1, :] += jnp.sum(low_query.astype(f32), axis=0, keepdims=True)

    @pl.when(step == blocks - 1)
    def _():
        cosine = widen(cos_ref[...], width)
        sine = widen(sin_ref[...], width)
        low_key = rotate(dk_all[...], cosine, -sine).astype(bf16)
        low_value = dv_all[...].astype(bf16)
        out_ref[:, width : 2 * width] = low_key
        out_ref[:, 2 * width :] = low_value
        sum_ref[1:2, :] = jnp.sum(low_key.astype(f32), axis=0, keepdims=True)
        sum_ref[2:3, :] = jnp.sum(low_value.astype(f32), axis=0, keepdims=True)


def attend_back(qkv, d_out, lse, mask, cosine, sine, low, rows):
    seq_len, width = d_out.shape
    blocks = seq_len // rows
    stat_rows = lse.shape[0]
    grid_spec = pltpu.PrefetchScalarGridSpec(
        num_scalar_prefetch=1,
        grid=(blocks,),
        in_specs=[
            pl.BlockSpec((1, rows, width), lambda i, low: (0, i, 0)),
            pl.BlockSpec((1, seq_len, width), lambda i, low: (1, 0, 0)),
            pl.BlockSpec((1, seq_len, width), lambda i, low: (2, 0, 0)),
            pl.BlockSpec((rows, width), lambda i, low: (i, 0)),
            pl.BlockSpec((stat_rows, rows), lambda i, low: (0, i)),
            pl.BlockSpec((seq_len, rows), lambda i, low: (0, i)),
            pl.BlockSpec((seq_len, LANES), lambda i, low: (0, 0)),
            pl.BlockSpec((seq_len, LANES), lambda i, low: (0, 0)),
        ],
        out_specs=[
            pl.BlockSpec((seq_len, 3 * width), lambda i, low: (0, 0)),
            pl.BlockSpec((8, width), lambda i, low: (0, 0)),
        ],
        scratch_shapes=[pltpu.VMEM((seq_len, width), f32), pltpu.VMEM((seq_len, width), f32)],
    )
    pairs = seq_len * seq_len * width
    return pl.pallas_call(
        attend_back_kernel,
        grid_spec=grid_spec,
        out_shape=[
            jax.ShapeDtypeStruct((seq_len, 3 * width), bf16),
            jax.ShapeDtypeStruct((8, width), f32),
        ],
        compiler_params=pltpu.CompilerParams(vmem_limit_bytes=32 * 1024 * 1024),
        cost_estimate=pl.CostEstimate(
            flops=10 * pairs, bytes_accessed=8 * seq_len * seq_len, transcendentals=pairs // HEAD_DIM
        ),
        name="attend_back",
    )(low, qkv, qkv, qkv, d_out, lse, mask, cosine, sine)


def adam_update(moments, gradient):
    first_fix = 1.0 - beta_first**STEP
    second_fix = 1.0 - beta_second**STEP
    moment_one = beta_first * moments[0] + (1.0 - beta_first) * gradient
    moment_two = beta_second * moments[1] + (1.0 - beta_second) * gradient * gradient
    scaled_step = moment_one / first_fix / (jnp.sqrt(moment_two / second_fix) + adam_eps)
    return (scaled_step, jnp.stack([moment_one, moment_two]))


def swap(array, distance):
    size = lax.axis_size("dp")
    return lax.ppermute(array, "dp", [(i, i ^ distance) for i in range(size)])


def after(array, *others):
    return lax.optimization_barrier((array, *others))[0]


def gather_pieces(own):
    size = lax.axis_size("dp")
    if size != 4:
        return [own] + [swap(own, j) for j in range(1, size)]
    half = own.shape[0] // 2
    near, far = swap(own, 1), swap(own, 2)
    top = swap(near[:half], 2)
    bottom = swap(far[half:], 1)
    return [own, near, far, jnp.concatenate([top, bottom], axis=0)]


def scatter_pieces(pieces):
    size = len(pieces)
    if size != 4:
        total = pieces[0].astype(f32)
        for j in range(1, size):
            total = total + swap(pieces[j], j).astype(f32)
        return total
    half = pieces[0].shape[0] // 2
    top = swap(pieces[3][:half], 1)
    bottom = swap(pieces[3][half:], 2)

    def plus(left, right):
        return (left.astype(f32) + right.astype(f32)).astype(bf16)

    near = swap(jnp.concatenate([pieces[1][:half], plus(pieces[1][half:], bottom)], axis=0), 1)
    far = swap(jnp.concatenate([plus(pieces[2][:half], top), pieces[2][half:]], axis=0), 2)
    return pieces[0].astype(f32) + near.astype(f32) + far.astype(f32)


def body(
    tokens,
    cotangent,
    segments,
    valid_mask,
    norm_params,
    norm_moments,
    heads_weight,
    heads_moments,
    heads_bias,
    heads_bias_moments,
    merge_weight,
    merge_moments,
    expand_weight,
    expand_moments,
    expand_bias,
    expand_bias_moments,
    shrink_weight,
    shrink_moments,
    output_bias,
    output_bias_moments,
):
    ranks = lax.axis_size("dp")
    rank = lax.axis_index("dp")
    count, _, model_width = tokens.shape
    seq_len = segments.shape[1]
    width = heads_weight.shape[2]
    piece = model_width // ranks
    rows = min(256, seq_len)

    def relative(array):
        parts = [
            lax.dynamic_slice_in_dim(array, (rank ^ j) * piece, piece, array.ndim - 1) for j in range(ranks)
        ]
        return jnp.concatenate(parts, axis=-1)

    heads_own = jnp.concatenate([heads_weight[c] for c in range(3)], axis=1).astype(bf16)
    heads_pieces = gather_pieces(heads_own)
    expand_pieces = gather_pieces(after(expand_weight.astype(bf16), heads_pieces[1], heads_pieces[2]))
    merge_pieces = gather_pieces(after(merge_weight.astype(bf16), expand_pieces[1], expand_pieces[2]))
    shrink_pieces = gather_pieces(after(shrink_weight.astype(bf16), merge_pieces[1], merge_pieces[2]))
    heads_full = jnp.concatenate(heads_pieces, axis=0)
    expand_full = jnp.concatenate(expand_pieces, axis=0)
    merge_full = jnp.concatenate(merge_pieces, axis=1)
    shrink_full = jnp.concatenate(shrink_pieces, axis=1)

    norm_rel = relative(norm_params)
    norm_gain, norm_shift = norm_rel[0], norm_rel[1]
    inputs = relative(tokens).astype(f32)
    cot_rows = relative(cotangent)
    row_mean = jnp.mean(inputs, axis=-1, keepdims=True)
    centred = inputs - row_mean
    variance = jnp.mean(centred * centred, axis=-1, keepdims=True)
    inv_std = lax.rsqrt(variance + norm_eps)
    unit = centred * inv_std
    normed_rows = (unit * norm_gain + norm_shift).astype(bf16)

    def gather_rows(array):
        return lax.all_gather(array, "tensor", axis=0, tiled=True)

    def scatter_rows(array):
        return lax.psum_scatter(array, "tensor", scatter_dimension=0, tiled=True)

    normed = [gather_rows(normed_rows[s]) for s in range(count)]
    cot = [gather_rows(after(cot_rows[s], normed_rows)) for s in range(count)]

    starts = [document_starts(segments[s]) for s in range(count)]
    tables = [rotary_tables(start) for start in starts]
    masked = [masks(starts[s], valid_mask[s]) for s in range(count)]
    lows = [start[::rows] // rows for start in starts]

    outs, kept = [], []
    for s in range(count):
        triple = nn(normed[s], heads_full)
        qkv, attended, lse = attend(triple, heads_bias, *tables[s], masked[s][0], lows[s], rows)
        pre = nn(normed[s], expand_full) + expand_bias
        inner = jnp.sqrt(2.0 / jnp.pi).astype(f32) * (pre + 0.044715 * pre * pre * pre)
        tanh = jnp.tanh(inner)
        hidden = (0.5 * pre * (1.0 + tanh)).astype(bf16)
        slope = 0.5 * (1.0 + tanh) + 0.5 * pre * (1.0 - tanh * tanh) * (
            jnp.sqrt(2.0 / jnp.pi).astype(f32) * (1.0 + 3 * 0.044715 * pre * pre)
        )
        hidden, slope = lax.optimization_barrier((hidden, slope.astype(bf16)))
        partial = (nn(attended, merge_full) + nn(hidden, shrink_full)).astype(bf16)
        outs.append(scatter_rows(partial))
        kept.append((qkv, attended, lse, hidden, slope))

    d_cats, d_hiddens, grads, bias_sums, hidden_sums = [], [], [], [], []
    for s in range(count):
        qkv, attended, lse, hidden, slope = kept[s]
        d_attended = nt(cot[s], merge_full).astype(bf16)
        d_cat, sums = attend_back(qkv, d_attended, lse, masked[s][1], *tables[s], lows[s], rows)
        d_hidden = (nt(cot[s], shrink_full) * slope.astype(f32)).astype(bf16)
        hidden_sums.append(jnp.sum(d_hidden.astype(f32), axis=0))
        partial = (nt(d_cat, heads_full) + nt(d_hidden, expand_full)).astype(bf16)
        grads.append(scatter_rows(partial))
        d_cats.append(d_cat)
        d_hiddens.append(d_hidden)
        bias_sums.append(sums[:3])

    normed_all = jnp.concatenate(normed, axis=0)
    cot_all = jnp.concatenate(cot, axis=0)
    d_cat_all = jnp.concatenate(d_cats, axis=0)
    d_hidden_all = jnp.concatenate(d_hiddens, axis=0)
    attended_all = jnp.concatenate([k[1] for k in kept], axis=0)
    hidden_all = jnp.concatenate([k[3] for k in kept], axis=0)

    def columns(array, j):
        return array[:, j * piece : (j + 1) * piece]

    order = list(range(ranks))[::-1]

    def spread(make):
        made = {j: make(j) for j in order}
        return scatter_pieces([made[j] for j in range(ranks)])

    shrink_grad = spread(lambda j: tn(hidden_all, columns(cot_all, j)).astype(bf16))
    merge_grad = spread(lambda j: tn(attended_all, columns(cot_all, j)).astype(bf16))
    expand_grad = spread(lambda j: tn(columns(normed_all, j), d_hidden_all).astype(bf16))
    heads_cat = spread(lambda j: tn(columns(normed_all, j), d_cat_all).astype(bf16))
    heads_grad = jnp.stack([heads_cat[:, c * width : (c + 1) * width] for c in range(3)])

    branches = jnp.stack(outs).astype(f32)
    bias_row = relative(output_bias[0] + output_bias[1])
    output = relative((inputs + branches + bias_row).astype(bf16))

    d_normed = jnp.stack(grads).astype(f32)
    cot_float = cot_rows.astype(f32)
    d_unit = d_normed * norm_gain
    mean_unit = jnp.mean(d_unit, axis=-1, keepdims=True)
    mean_cross = jnp.mean(d_unit * unit, axis=-1, keepdims=True)
    input_grad = relative((cot_float + inv_std * (d_unit - mean_unit - unit * mean_cross)).astype(bf16))

    norm_step = relative(
        jnp.stack([jnp.sum(d_normed * unit, axis=(0, 1)), jnp.sum(d_normed, axis=(0, 1))])
    )
    output_bias_step = relative(jnp.sum(cot_float, axis=(0, 1)))
    heads_bias_total, expand_bias_total = lax.psum((sum(bias_sums), sum(hidden_sums)), "dp")
    norm_total, output_bias_total = lax.psum((norm_step, output_bias_step), ("dp", "tensor"))

    scale_back = 1.0 / seq_len
    norm_upd, norm_mom = adam_update(norm_moments, norm_total * scale_back)
    heads_upd, heads_mom = adam_update(heads_moments, heads_grad * scale_back)
    hbias_upd, hbias_mom = adam_update(heads_bias_moments, heads_bias_total * scale_back)
    merge_upd, merge_mom = adam_update(merge_moments, merge_grad * scale_back)
    expand_upd, expand_mom = adam_update(expand_moments, expand_grad * scale_back)
    ebias_upd, ebias_mom = adam_update(expand_bias_moments, expand_bias_total * scale_back)
    shrink_upd, shrink_mom = adam_update(shrink_moments, shrink_grad * scale_back)
    output_bias_grad = jnp.stack([output_bias_total, output_bias_total]) * scale_back
    obias_upd, obias_mom = adam_update(output_bias_moments, output_bias_grad)
    return (
        output,
        input_grad,
        norm_upd,
        norm_mom,
        heads_upd,
        heads_mom,
        hbias_upd,
        hbias_mom,
        merge_upd,
        merge_mom,
        expand_upd,
        expand_mom,
        ebias_upd,
        ebias_mom,
        shrink_upd,
        shrink_mom,
        obias_upd,
        obias_mom,
    )


def solution(mesh):
    placed = (
        P("dp", "tensor", None),
        P("dp", "tensor", None),
        P("dp", None),
        P("dp", None),
        P(),
        P(),
        P(None, "dp", "tensor"),
        P(None, None, "dp", "tensor"),
        P(None, "tensor"),
        P(None, None, "tensor"),
        P("tensor", "dp"),
        P(None, "tensor", "dp"),
        P("dp", "tensor"),
        P(None, "dp", "tensor"),
        P("tensor"),
        P(None, "tensor"),
        P("tensor", "dp"),
        P(None, "tensor", "dp"),
        P(),
        P(),
    )
    return jax.shard_map(
        body,
        mesh=mesh,
        in_specs=placed,
        out_specs=(placed[0], placed[0], P(), P(), *placed[6:18], P(), P()),
        check_vma=False,
    )
```

time: 1190 us -> 520 us (0.44)
  waiting for transfers between devices: 653 us -> 116 us
  matrix products: 224 us -> 144 us
  other arithmetic: 113 us -> 58.4 us
  local copies, waits for them, and re-layouts: 107 us -> 52.4 us
  Pallas kernels: 0 us -> 43.2 us
  starting transfers between devices: 0.84 us -> 37.2 us
  loops' own time: 25.6 us -> 0 us
    reduce_scatter x12 -> x4, waiting for transfers between devices: 359 us -> 0.04 us  [scatter_rows(): return lax.psum_scatter(array, 'tensor', scatter_dimension=0, tiled=True)]
    all_gather x8 -> x4, waiting for transfers between devices: 294 us -> 1.86 us  [gather_rows(): return lax.all_gather(array, 'tensor', axis=0, tiled=True)]
    ppermute x0 -> x32, waiting for transfers between devices: none -> 113 us  [swap(): return lax.ppermute(array, 'dp', [(i, i ^ distance) for i in range(size)])]
    dot_general x52 -> x32, matrix products: 224 us -> 144 us  [the longest x8 56.1 us: nn(): lax.dot_general(left, right, (((1,), (0,)), ((), ())), preferred_element_...]
    while x253 -> x0, local copies, waits for them, and re-layouts: 44.7 us -> none
    dynamic_update_slice x8 -> x0, local copies, waits for them, and re-layouts: 43.7 us -> none  [micro_step(): attended_blocks, log_totals = lax.map(attend, (query_blocks, block_starts))]
    pallas_call x0 -> x4, Pallas kernels: none -> 43.2 us  [the longest x2 28.3 us: attend_back(): pl.pallas_call(attend_back_kernel, grid_spec=grid_spec, out_shape=[jax.Sh...]
    ppermute x0 -> x32, starting transfers between devices: none -> 36.9 us  [swap(): return lax.ppermute(array, 'dp', [(i, i ^ distance) for i in range(size)])]
  transfers between devices with their start and end apart: 20 -> 40, of which waited for: 17 -> 16; matrix products, arithmetic and copies ran while one was open for 20% -> 43% of each run, Pallas kernels for 0% -> 8%
where the time goes in v1:
time: 520 us; the launch traced here: 515 us
  matrix products  144 us (28%)
  waiting for transfers between devices  116 us (22%)
  other arithmetic  58.4 us (11%)
  local copies, waits for them, and re-layouts  52.4 us (10%)
  blocking collectives  47.7 us (9%)
  Pallas kernels  43.2 us (8%)
  starting transfers between devices  37.2 us (7%)
  between operations  16.6 us (3%)
    ppermute x32, waiting for transfers between devices, swap(): return lax.ppermute(array, 'dp', [(i, i ^ distance) for i in range(size)])  113 us
    dot_general x8, matrix products, nn(): lax.dot_general(left, right, (((1,), (0,)), ((), ())), preferred_element_...  56.1 us
    dot_general x8, matrix products, nt(): lax.dot_general(left, right, (((1,), (1,)), ((), ())), preferred_element_...  46.1 us
    dot_general x16, matrix products, tn(): lax.dot_general(left, right, (((0,), (0,)), ((), ())), preferred_element_...  41.6 us
    psum x1, blocking collectives, body(): lax.psum((norm_step, output_bias_step), ('dp', 'tensor'))  38 us
    ppermute x32, starting transfers between devices, swap(): return lax.ppermute(array, 'dp', [(i, i ^ distance) for i in range(size)])  36.9 us
    unnamed x296, local copies, waits for them, and re-layouts  30.2 us
    pallas_call x2, Pallas kernels, attend_back(): pl.pallas_call(attend_back_kernel, grid_spec=grid_spec, out_shape=[jax.Sh...  28.3 us
  transfers between devices with their start and end apart: 40, of which 16 were waited for; matrix products, arithmetic and copies ran while one was open for 43% of the time, Pallas kernels for 8%

profile of v1, /device:TPU:0, one launch (start us, length us, event | category | flops | bytes accessed | tf_op | source)
XLA Modules:
  0.0 515.4 jit_solution(4151947688349491573)
XLA Ops:
  24.0 14.7 %collective-permute-done = bf16[512,768]{1,0:T(8,128)(2,1)} collective-permute-done((bf16[512,768]{1,0:T(8,128)(2,1)}, bf16[512,768]{1,0:T(8,128)(2,1)}, u32[]{:S(2)}, u32[]{:S(2)}) %collective-permute-start) | collective-permute-done | bytes 786464 | tf_op jit(solution)/shard_map/ppermute | solution.py:285
  44.9 4.9 select_convert_fusion.1
  49.9 14.0 %collective-permute-done.4 = bf16[512,1024]{1,0:T(8,128)(2,1)S(1)} collective-permute-done((bf16[512,1024]{1,0:T(8,128)(2,1)S(1)}, bf16[512,1024]{1,0:T(8,128)(2,1)S(1)}, u32[]{:S(2)}, u32[]{:S(2)}) %collective-permute-start.4) | collective-permute-done | bytes 1048608 | tf_op jit(solution)/shard_map/ppermute | solution.py:285
  92.9 25.7 %collective-permute-done.10 = bf16[256,1024]{1,0:T(8,128)(2,1)S(1)} collective-permute-done((bf16[256,1024]{1,0:T(8,128)(2,1)S(1)}, bf16[256,1024]{1,0:T(8,128)(2,1)S(1)}, u32[]{:S(2)}, u32[]{:S(2)}) %collective-permute-start.10) | collective-permute-done | bytes 524320 | tf_op jit(solution)/shard_map/ppermute | solution.py:285
  124.4 10.0 %fusion.114 = f32[1024,1024]{1,0:T(8,128)} fusion(bf16[2048,1024]{1,0:T(8,128)(2,1)} %copy-done.94, bf16[1,1024,2048]{2,1,0:T(8,128)(2,1)} %all-gather.13.cloned.1.call-done), kind=kOutput, calls=%fused_computation.321 | convolution fusion | flops 4294967296 | bytes 12582912 | tf_op jit(solution)/shard_map/dot_general | solution.py:70
  134.5 15.1 %fusion.6 = (bf16[1024,1024]{1,0:T(8,128)(2,1)}, bf16[1024,1024]{1,0:T(8,128)(2,1)}, bf16[1024,1024]{1,0:T(8,128)(2,1)}, bf16[1024,1024]{1,0:T(8,128)(2,1)}) fusion(f32[1024]{0:T(1024)S(1)} %copy-done.129, f32[1024,1024]{1,0:T(8,128)} %fusion.114, bf16[2048,1024]{1,0:T(8,128)(2,1)} %copy-done.94, bf16[1,1024,2048]{2,1,0:T(8,128)(2,1)} %all-gather.11.cloned.1.call-done), kind=kOutput, calls=%fused_computation.20 | convolution fusion | flops 4339007488 | bytes 20975616 | tf_op jit(solution)/shard_map/dot_general | solution.py:70
  149.6 5.1 fusion.120.triple_ref
  161.6 7.0 %attend.2 = (bf16[3,1024,256]{2,1,0:T(8,128)(2,1)S(1)}, bf16[1024,256]{1,0:T(8,128)(2,1)S(1)}, f32[8,1024]{1,0:T(8,128)S(1)}) custom-call(s32[4]{0:T(128)S(1)} %and_select_fusion.1.low_ref, f32[1024,768]{1,0:T(8,128)S(1)} %copy-done.12, f32[3,256]{1,0:T(4,128)S(1)} %copy-done.11, f32[1024,128]{1,0:T(8,128)S(1)} %copy-done.5, f32[1024,128]{1,0:T(8,128)S(1)} %copy.42.sin_ref, ...), custom_call_target="tpu_custom_call" | custom-call | flops 1073741824 | bytes 8388608 | tf_op jit(solution)/shard_map/attend/pallas_call | solution.py:149
  168.6 13.2 %attend_back.2 = (bf16[1024,768]{1,0:T(8,128)(2,1)S(1)}, f32[8,256]{1,0:T(8,128)S(1)}) custom-call(s32[4]{0:T(128)S(1)} %and_select_fusion.1.low_ref, bf16[3,1024,256]{2,1,0:T(8,128)(2,1)S(1)} %get-tuple-element.44.q_ref.k_ref.v_ref, bf16[3,1024,256]{2,1,0:T(8,128)(2,1)S(1)} %get-tuple-element.44.q_ref.k_ref.v_ref, ...), custom_call_target="tpu_custom_call" | custom-call | flops 2684354560 | bytes 8388608 | tf_op jit(solution)/shard_map/attend_back/pallas_call | solution.py:259
  181.9 7.4 %convert_reduce_fusion.1 = (f32[1024]{0:T(1024)S(1)}, bf16[1024,1024]{1,0:T(8,128)(2,1)S(1)}) fusion(bf16[1024,1024]{1,0:T(8,128)(2,1)S(1)} %copy-done.139, bf16[1024,2048]{1,0:T(8,128)(2,1)S(1)} %copy-done.40, bf16[512,512]{1,0:T(8,128)(2,1)} %collective-permute-done.15, bf16[512,512]{1,0:T(8,128)(2,1)} %collective-permute-done.14, ...), kind=kOutput, calls=%fused_computation.33 | convolution fusion | flops 4321180672 | bytes 12587008 | tf_op jit(solution)/shard_map/dot_general | solution.py:66
  189.4 4.6 fusion.147
  194.0 5.1 add_convert_fusion.1
  206.3 5.4 %fusion.116.triple_ref = f32[1024,768]{1,0:T(8,128)S(1)} fusion(bf16[2048,768]{1,0:T(8,128)(2,1)} %constant_dynamic-update-slice_fusion, bf16[1,1024,2048]{2,1,0:T(8,128)(2,1)S(1)} %copy-done.30), kind=kOutput, calls=%fused_computation.323 | convolution fusion | flops 3221225472 | bytes 10485760 | tf_op jit(solution)/shard_map/dot_general | solution.py:70
  211.7 8.0 %attend.3 = (bf16[3,1024,256]{2,1,0:T(8,128)(2,1)S(1)}, bf16[1024,256]{1,0:T(8,128)(2,1)S(1)}, f32[8,1024]{1,0:T(8,128)S(1)}) custom-call(s32[4]{0:T(128)S(1)} %and_select_fusion.low_ref, f32[1024,768]{1,0:T(8,128)S(1)} %fusion.116.triple_ref, f32[3,256]{1,0:T(4,128)S(1)} %copy-done.11, f32[1024,128]{1,0:T(8,128)S(1)} %copy-done.9, ...), custom_call_target="tpu_custom_call" | custom-call | flops 1073741824 | bytes 8388608 | tf_op jit(solution)/shard_map/attend/pallas_call | solution.py:149
  224.8 15.1 %attend_back.3 = (bf16[1024,768]{1,0:T(8,128)(2,1)S(1)}, f32[8,256]{1,0:T(8,128)S(1)}) custom-call(s32[4]{0:T(128)S(1)} %and_select_fusion.low_ref, bf16[3,1024,256]{2,1,0:T(8,128)(2,1)S(1)} %copy-done.14, bf16[3,1024,256]{2,1,0:T(8,128)(2,1)S(1)} %copy-done.14, bf16[3,1024,256]{2,1,0:T(8,128)(2,1)S(1)} %copy-done.14, ...), custom_call_target="tpu_custom_call" | custom-call | flops 2684354560 | bytes 8388608 | tf_op jit(solution)/shard_map/attend_back/pallas_call | solution.py:259
  240.0 7.0 %convert_reduce_fusion = (f32[1024]{0:T(1024)S(1)}, bf16[1024,1024]{1,0:T(8,128)(2,1)S(1)}) fusion(bf16[1024,1024]{1,0:T(8,128)(2,1)S(1)} %copy-done.138, bf16[1024,2048]{1,0:T(8,128)(2,1)S(1)} %copy-done.42, bf16[512,512]{1,0:T(8,128)(2,1)} %collective-permute-done.15, bf16[512,512]{1,0:T(8,128)(2,1)} %collective-permute-done.14, ...), kind=kOutput, calls=%fused_computation.32 | convolution fusion | flops 4321180672 | bytes 12587008 | tf_op jit(solution)/shard_map/dot_general | solution.py:66
  247.1 7.0 %fusion.148 = f32[1024,2048]{1,0:T(8,128)} fusion(bf16[1024,1024]{1,0:T(8,128)(2,1)S(1)} %get-tuple-element.221, bf16[2048,1024]{1,0:T(8,128)(2,1)S(1)} %copy-done.96), kind=kOutput, calls=%fused_computation.349 | convolution fusion | flops 4294967296 | bytes 14680064 | tf_op jit(solution)/shard_map/dot_general | solution.py:66
  254.1 7.3 %add_convert_fusion = bf16[1024,2048]{1,0:T(8,128)(2,1)} fusion(f32[1024,2048]{1,0:T(8,128)} %fusion.148, bf16[1024,768]{1,0:T(8,128)(2,1)S(1)} %get-tuple-element.52, bf16[2048,768]{1,0:T(8,128)(2,1)S(1)} %copy-done.111), kind=kOutput, calls=%fused_computation.6 | convolution fusion | flops 3225419776 | bytes 17301504 | tf_op jit(solution)/shard_map/dot_general | solution.py:66
  289.6 5.8 %fusion.138 = f32[1024,2048]{1,0:T(8,128)S(1)} fusion(bf16[1024,1024]{1,0:T(8,128)(2,1)S(1)} %copy-done.54, bf16[512,512]{1,0:T(8,128)(2,1)} %collective-permute-done.15, bf16[512,512]{1,0:T(8,128)(2,1)} %collective-permute-done.14, bf16[1024,512]{1,0:T(8,128)(2,1)S(1)} %copy-done.105, bf16[1024,512]{1,0:T(8,128)(2,1)S(1)} %copy-done.100, ...), kind=kOutput, calls=%fused_computation.339 | convolution fusion | flops 4315938816 | bytes 14680064 | tf_op jit(solution)/shard_map/dot_general | solution.py:70
  295.5 4.4 add_convert_fusion.3
  299.9 5.4 %convolution_convert_fusion.2 = bf16[512,1024]{1,0:T(8,128)(2,1)S(1)} fusion(bf16[1024,1024]{1,0:T(8,128)(2,1)} %copy-done.134, bf16[1024,1024]{1,0:T(8,128)(2,1)} %copy-done.130, bf16[1024,2048]{1,0:T(8,128)(2,1)} %bitcast.227, bf16[1024,2048]{1,0:T(8,128)(2,1)} %bitcast.220), kind=kOutput, calls=%fused_computation.136 | convolution fusion | flops 2160590848 | bytes 13631488 | tf_op jit(solution)/shard_map/dot_general | solution.py:74
  316.8 9.7 %all-reduce.1 = (f32[3,256]{1,0:T(4,128)S(1)}, f32[1024]{0:T(1024)S(1)}) all-reduce(f32[3,256]{1,0:T(4,128)S(1)} %slice_add_fusion.1, f32[1024]{0:T(1024)S(1)} %add.370), channel_id=1, replica_groups=mesh['dp'=4,'tensor'=8] {'dp'}, use_global_device_ids=true, to_apply=%region_15.16 | all-reduce | flops 1792 | bytes 14336 | tf_op jit(solution)/shard_map/psum | solution.py:459
  330.1 4.1 convolution_convert_fusion.6
  347.0 5.8 %fusion.137 = f32[1024,2048]{1,0:T(8,128)S(1)} fusion(bf16[1024,1024]{1,0:T(8,128)(2,1)S(1)} %copy-done.53, bf16[512,512]{1,0:T(8,128)(2,1)} %collective-permute-done.15, bf16[512,512]{1,0:T(8,128)(2,1)} %collective-permute-done.14, bf16[1024,512]{1,0:T(8,128)(2,1)S(1)} %copy-done.106, bf16[1024,512]{1,0:T(8,128)(2,1)S(1)} %copy-done.101, ...), kind=kOutput, calls=%fused_computation.338 | convolution fusion | flops 4315938816 | bytes 14680064 | tf_op jit(solution)/shard_map/dot_general | solution.py:70
  352.8 4.4 add_convert_fusion.2
  357.2 5.3 %fusion.67 = bf16[1024,512]{1,0:T(8,128)(2,1)S(1)} fusion(bf16[2048,1024]{1,0:T(8,128)(2,1)} %copy-done.75, bf16[2048,2048]{1,0:T(8,128)(2,1)} %copy-done.51), kind=kOutput, calls=%fused_computation.130 | convolution fusion | flops 2148007936 | bytes 7340032 | tf_op jit(solution)/shard_map/dot_general | solution.py:74
  368.1 5.1 collective-permute-done.16
  382.6 11.8 %collective-permute-done.18 = bf16[256,768]{1,0:T(8,128)(2,1)S(1)} collective-permute-done((bf16[256,768]{1,0:T(8,128)(2,1)S(1)}, bf16[256,768]{1,0:T(8,128)(2,1)S(1)}, u32[]{:S(2)}, u32[]{:S(2)}) %collective-permute-start.18) | collective-permute-done | bytes 393248 | tf_op jit(solution)/shard_map/ppermute | solution.py:285
  405.2 9.8 %collective-permute-done.17 = bf16[512,768]{1,0:T(8,128)(2,1)S(1)} collective-permute-done((bf16[512,768]{1,0:T(8,128)(2,1)S(1)}, bf16[512,768]{1,0:T(8,128)(2,1)S(1)}, u32[]{:S(2)}, u32[]{:S(2)}) %collective-permute-start.17) | collective-permute-done | bytes 786464 | tf_op jit(solution)/shard_map/ppermute | solution.py:285
  425.2 12.3 %collective-permute-done.29 = bf16[1024,512]{1,0:T(8,128)(2,1)S(1)} collective-permute-done((bf16[1024,512]{1,0:T(8,128)(2,1)S(1)}, bf16[1024,512]{1,0:T(8,128)(2,1)S(1)}, u32[]{:S(2)}, u32[]{:S(2)}) %collective-permute-start.29) | collective-permute-done | bytes 1048608 | tf_op jit(solution)/shard_map/ppermute | solution.py:285
  445.1 9.6 %collective-permute-done.25 = bf16[512,1024]{1,0:T(8,128)(2,1)S(1)} collective-permute-done((bf16[512,1024]{1,0:T(8,128)(2,1)S(1)}, bf16[512,1024]{1,0:T(8,128)(2,1)S(1)}, u32[]{:S(2)}, u32[]{:S(2)}) %collective-permute-start.25) | collective-permute-done | bytes 1048608 | tf_op jit(solution)/shard_map/ppermute | solution.py:285
  462.6 38.0 %all-reduce = (f32[2,2048]{1,0:T(2,128)S(1)}, f32[2048]{0:T(1024)S(1)}) all-reduce(f32[2,2048]{1,0:T(2,128)S(1)} %pad_maximum_fusion.25, f32[2048]{0:T(1024)S(1)} %copy-done.118), channel_id=1, replica_groups=mesh['dp'=4,'tensor'=8] {'dp','tensor'}, use_global_device_ids=true, to_apply=%region_14.15 | all-reduce | flops 6144 | bytes 49152 | tf_op jit(solution)/shard_map/psum | solution.py:460
  (533 shorter events, 190.7 us)
Async XLA Ops:
  7.2 117.2 %all-gather.13.cloned.1.call-start = ((), (), s32[]{:S(2)}) async-start(), calls=%async_computation.11 | async-start | bytes 4718592 | tf_op jit(solution)/shard_map/all_gather | solution.py:380
  11.0 123.4 %all-gather.11.cloned.1.call-start = ((), (), s32[]{:S(2)}) async-start(), calls=%async_computation.10 | async-start | bytes 4718592 | tf_op jit(solution)/shard_map/all_gather | solution.py:380
  11.8 144.8 %all-gather.7.cloned.1.call-start = ((), (), s32[]{:S(2)}) async-start(), calls=%async_computation.6 | async-start | bytes 4718592 | tf_op jit(solution)/shard_map/all_gather | solution.py:380
  14.9 205.9 %all-gather.9.cloned.1.call-start = ((), (), s32[]{:S(2)}) async-start(), calls=%async_computation.8 | async-start | bytes 4718592 | tf_op jit(solution)/shard_map/all_gather | solution.py:380
  17.9 20.8 %collective-permute-start = (bf16[512,768]{1,0:T(8,128)(2,1)}, bf16[512,768]{1,0:T(8,128)(2,1)}, u32[]{:S(2)}, u32[]{:S(2)}) collective-permute-start(bf16[512,768]{1,0:T(8,128)(2,1)} %get-tuple-element.163), channel_id=1, source_target_pairs={{0,8},{8,0},{16,24},{24,16},{1,9},{9,1},{17,25},{25,17},{2,10},{10... | collective-permute-start | bytes 2359304 | tf_op jit(solution)/shard_map/ppermute | solution.py:285
  20.9 19.3 %collective-permute-start.1 = (bf16[512,768]{1,0:T(8,128)(2,1)}, bf16[512,768]{1,0:T(8,128)(2,1)}, u32[]{:S(2)}, u32[]{:S(2)}) collective-permute-start(bf16[512,768]{1,0:T(8,128)(2,1)} %get-tuple-element.163), channel_id=1, source_target_pairs={{0,16},{8,24},{16,0},{24,8},{1,17},{9,25},{17,1},{25,9},{2,18},{10... | collective-permute-start | bytes 2359304 | tf_op jit(solution)/shard_map/ppermute | solution.py:285
  22.4 437.7 %reduce-scatter.9.cloned.1.call-start = ((), (), s32[]{:S(2)}) async-start(), calls=%async_computation.7 | async-start | bytes 4718592 | tf_op jit(solution)/shard_map/reduce_scatter | solution.py:383
  40.2 23.7 %collective-permute-start.4 = (bf16[512,1024]{1,0:T(8,128)(2,1)S(1)}, bf16[512,1024]{1,0:T(8,128)(2,1)S(1)}, u32[]{:S(2)}, u32[]{:S(2)}) collective-permute-start(bf16[512,1024]{1,0:T(8,128)(2,1)S(1)} %convert_element_type.266), channel_id=1, source_target_pairs={{0,8},{8,0},{16,24},{24,16},{1,9},{9,1},{17,25},{25,17},{2,10},{10... | collective-permute-start | bytes 3145736 | tf_op jit(solution)/shard_map/ppermute | solution.py:285
  40.5 23.7 %collective-permute-start.5 = (bf16[512,1024]{1,0:T(8,128)(2,1)S(1)}, bf16[512,1024]{1,0:T(8,128)(2,1)S(1)}, u32[]{:S(2)}, u32[]{:S(2)}) collective-permute-start(bf16[512,1024]{1,0:T(8,128)(2,1)S(1)} %convert_element_type.266), channel_id=1, source_target_pairs={{0,16},{8,24},{16,0},{24,8},{1,17},{9,25},{17,1},{25,9},{2,18},{10... | collective-permute-start | bytes 3145736 | tf_op jit(solution)/shard_map/ppermute | solution.py:285
  77.8 42.2 %collective-permute-start.12 = (bf16[1024,512]{1,0:T(8,128)(2,1)S(1)}, bf16[1024,512]{1,0:T(8,128)(2,1)S(1)}, u32[]{:S(2)}, u32[]{:S(2)}) collective-permute-start(bf16[1024,512]{1,0:T(8,128)(2,1)S(1)} %convert_element_type.269), channel_id=1, source_target_pairs={{0,8},{8,0},{16,24},{24,16},{1,9},{9,1},{17,25},{25,17},{2,10},{10... | collective-permute-start | bytes 3145736 | tf_op jit(solution)/shard_map/ppermute | solution.py:285
  78.6 43.8 %collective-permute-start.13 = (bf16[1024,512]{1,0:T(8,128)(2,1)S(1)}, bf16[1024,512]{1,0:T(8,128)(2,1)S(1)}, u32[]{:S(2)}, u32[]{:S(2)}) collective-permute-start(bf16[1024,512]{1,0:T(8,128)(2,1)S(1)} %convert_element_type.269), channel_id=1, source_target_pairs={{0,16},{8,24},{16,0},{24,8},{1,17},{9,25},{17,1},{25,9},{2,18},{10... | collective-permute-start | bytes 3145736 | tf_op jit(solution)/shard_map/ppermute | solution.py:285
  82.3 36.3 %collective-permute-start.10 = (bf16[256,1024]{1,0:T(8,128)(2,1)S(1)}, bf16[256,1024]{1,0:T(8,128)(2,1)S(1)}, u32[]{:S(2)}, u32[]{:S(2)}) collective-permute-start(bf16[256,1024]{1,0:T(8,128)(2,1)S(1)} %slice.370), channel_id=1, source_target_pairs={{0,16},{8,24},{16,0},{24,8},{1,17},{9,25},{17,1},{25,9},{2,18},{10... | collective-permute-start | bytes 1572872 | tf_op jit(solution)/shard_map/ppermute | solution.py:285
  87.8 32.1 %collective-permute-start.11 = (bf16[256,1024]{1,0:T(8,128)(2,1)S(1)}, bf16[256,1024]{1,0:T(8,128)(2,1)S(1)}, u32[]{:S(2)}, u32[]{:S(2)}) collective-permute-start(bf16[256,1024]{1,0:T(8,128)(2,1)S(1)} %slice.371), channel_id=1, source_target_pairs={{0,8},{8,0},{16,24},{24,16},{1,9},{9,1},{17,25},{25,17},{2,10},{10... | collective-permute-start | bytes 1572872 | tf_op jit(solution)/shard_map/ppermute | solution.py:285
  90.8 64.0 %collective-permute-start.8 = (bf16[128,512]{1,0:T(8,128)(2,1)S(1)}, bf16[128,512]{1,0:T(8,128)(2,1)S(1)}, u32[]{:S(2)}, u32[]{:S(2)}) collective-permute-start(bf16[128,512]{1,0:T(8,128)(2,1)S(1)} %slice.368), channel_id=1, source_target_pairs={{0,16},{8,24},{16,0},{24,8},{1,17},{9,25},{17,1},{25,9},{2,18},{10... | collective-permute-start | bytes 393224 | tf_op jit(solution)/shard_map/ppermute | solution.py:285
  118.6 36.1 %collective-permute-start.9 = (bf16[128,512]{1,0:T(8,128)(2,1)S(1)}, bf16[128,512]{1,0:T(8,128)(2,1)S(1)}, u32[]{:S(2)}, u32[]{:S(2)}) collective-permute-start(bf16[128,512]{1,0:T(8,128)(2,1)S(1)} %slice.369), channel_id=1, source_target_pairs={{0,8},{8,0},{16,24},{24,16},{1,9},{9,1},{17,25},{25,17},{2,10},{10... | collective-permute-start | bytes 393224 | tf_op jit(solution)/shard_map/ppermute | solution.py:285
  120.9 60.9 %collective-permute-start.14 = (bf16[512,512]{1,0:T(8,128)(2,1)}, bf16[512,512]{1,0:T(8,128)(2,1)}, u32[]{:S(2)}, u32[]{:S(2)}) collective-permute-start(bf16[512,512]{1,0:T(8,128)(2,1)} %slice.372), channel_id=1, source_target_pairs={{0,16},{8,24},{16,0},{24,8},{1,17},{9,25},{17,1},{25,9},{2,18},{10... | collective-permute-start | bytes 1572872 | tf_op jit(solution)/shard_map/ppermute | solution.py:285
  123.6 58.3 %collective-permute-start.15 = (bf16[512,512]{1,0:T(8,128)(2,1)}, bf16[512,512]{1,0:T(8,128)(2,1)}, u32[]{:S(2)}, u32[]{:S(2)}) collective-permute-start(bf16[512,512]{1,0:T(8,128)(2,1)} %slice.373), channel_id=1, source_target_pairs={{0,8},{8,0},{16,24},{24,16},{1,9},{9,1},{17,25},{25,17},{2,10},{10... | collective-permute-start | bytes 1572872 | tf_op jit(solution)/shard_map/ppermute | solution.py:285
  199.1 261.0 %reduce-scatter.11.cloned.1.call-start = ((), (), s32[]{:S(2)}) async-start(), calls=%async_computation.9 | async-start | bytes 4718592 | tf_op jit(solution)/shard_map/reduce_scatter | solution.py:383
  261.5 239.9 %reduce-scatter.5.cloned.1.call-start = ((), (), s32[]{:S(2)}) async-start(), calls=%async_computation.4 | async-start | bytes 4718592 | tf_op jit(solution)/shard_map/reduce_scatter | solution.py:383
  275.7 120.6 %collective-permute-start.28 = (bf16[512,512]{1,0:T(8,128)(2,1)}, bf16[512,512]{1,0:T(8,128)(2,1)}, u32[]{:S(2)}, u32[]{:S(2)}) collective-permute-start(bf16[512,512]{1,0:T(8,128)(2,1)} %get-tuple-element.134), channel_id=1, source_target_pairs={{0,16},{8,24},{16,0},{24,8},{1,17},{9,25},{17,1},{25,9},{2,18},{10... | collective-permute-start | bytes 1572872 | tf_op jit(solution)/shard_map/ppermute | solution.py:285
  279.0 119.6 %collective-permute-start.30 = (bf16[512,512]{1,0:T(8,128)(2,1)}, bf16[512,512]{1,0:T(8,128)(2,1)}, u32[]{:S(2)}, u32[]{:S(2)}) collective-permute-start(bf16[512,512]{1,0:T(8,128)(2,1)} %get-tuple-element.135), channel_id=1, source_target_pairs={{0,8},{8,0},{16,24},{24,16},{1,9},{9,1},{17,25},{25,17},{2,10},{10... | collective-permute-start | bytes 1572872 | tf_op jit(solution)/shard_map/ppermute | solution.py:285
  287.6 113.4 %collective-permute-start.24 = (bf16[256,1024]{1,0:T(8,128)(2,1)}, bf16[256,1024]{1,0:T(8,128)(2,1)}, u32[]{:S(2)}, u32[]{:S(2)}) collective-permute-start(bf16[256,1024]{1,0:T(8,128)(2,1)} %get-tuple-element.136), channel_id=1, source_target_pairs={{0,16},{8,24},{16,0},{24,8},{1,17},{9,25},{17,1},{25,9},{2,18},{10... | collective-permute-start | bytes 1572872 | tf_op jit(solution)/shard_map/ppermute | solution.py:285
  299.9 201.5 %reduce-scatter.7.cloned.1.call-start = ((), (), s32[]{:S(2)}) async-start(), calls=%async_computation.5 | async-start | bytes 4718592 | tf_op jit(solution)/shard_map/reduce_scatter | solution.py:383
  313.4 50.5 %collective-permute-start.20 = (bf16[128,512]{1,0:T(8,128)(2,1)}, bf16[128,512]{1,0:T(8,128)(2,1)}, u32[]{:S(2)}, u32[]{:S(2)}) collective-permute-start(bf16[128,512]{1,0:T(8,128)(2,1)} %get-tuple-element.167), channel_id=1, source_target_pairs={{0,16},{8,24},{16,0},{24,8},{1,17},{9,25},{17,1},{25,9},{2,18},{10... | collective-permute-start | bytes 393224 | tf_op jit(solution)/shard_map/ppermute | solution.py:285
  314.2 51.2 %collective-permute-start.22 = (bf16[128,512]{1,0:T(8,128)(2,1)}, bf16[128,512]{1,0:T(8,128)(2,1)}, u32[]{:S(2)}, u32[]{:S(2)}) collective-permute-start(bf16[128,512]{1,0:T(8,128)(2,1)} %get-tuple-element.168), channel_id=1, source_target_pairs={{0,8},{8,0},{16,24},{24,16},{1,9},{9,1},{17,25},{25,17},{2,10},{10... | collective-permute-start | bytes 393224 | tf_op jit(solution)/shard_map/ppermute | solution.py:285
  374.0 29.7 %collective-permute-start.26 = (bf16[256,1024]{1,0:T(8,128)(2,1)S(1)}, bf16[256,1024]{1,0:T(8,128)(2,1)S(1)}, u32[]{:S(2)}, u32[]{:S(2)}) collective-permute-start(bf16[256,1024]{1,0:T(8,128)(2,1)S(1)} %copy-done.89), channel_id=1, source_target_pairs={{0,8},{8,0},{16,24},{24,16},{1,9},{9,1},{17,25},{25,17},{2,10},{10... | collective-permute-start | bytes 1572872 | tf_op jit(solution)/shard_map/ppermute | solution.py:285
  394.5 20.5 %collective-permute-start.17 = (bf16[512,768]{1,0:T(8,128)(2,1)S(1)}, bf16[512,768]{1,0:T(8,128)(2,1)S(1)}, u32[]{:S(2)}, u32[]{:S(2)}) collective-permute-start(bf16[512,768]{1,0:T(8,128)(2,1)S(1)} %pad_maximum_fusion.18), channel_id=1, source_target_pairs={{0,8},{8,0},{16,24},{24,16},{1,9},{9,1},{17,25},{25,17},{2,10},{10... | collective-permute-start | bytes 2359304 | tf_op jit(solution)/shard_map/ppermute | solution.py:285
  396.2 20.5 %collective-permute-start.19 = (bf16[512,768]{1,0:T(8,128)(2,1)S(1)}, bf16[512,768]{1,0:T(8,128)(2,1)S(1)}, u32[]{:S(2)}, u32[]{:S(2)}) collective-permute-start(bf16[512,768]{1,0:T(8,128)(2,1)S(1)} %pad_maximum_fusion.19), channel_id=1, source_target_pairs={{0,16},{8,24},{16,0},{24,8},{1,17},{9,25},{17,1},{25,9},{2,18},{10... | collective-permute-start | bytes 2359304 | tf_op jit(solution)/shard_map/ppermute | solution.py:285
  398.6 38.8 %collective-permute-start.29 = (bf16[1024,512]{1,0:T(8,128)(2,1)S(1)}, bf16[1024,512]{1,0:T(8,128)(2,1)S(1)}, u32[]{:S(2)}, u32[]{:S(2)}) collective-permute-start(bf16[1024,512]{1,0:T(8,128)(2,1)S(1)} %pad_maximum_fusion.15), channel_id=1, source_target_pairs={{0,8},{8,0},{16,24},{24,16},{1,9},{9,1},{17,25},{25,17},{2,10},{10... | collective-permute-start | bytes 3145736 | tf_op jit(solution)/shard_map/ppermute | solution.py:285
  401.0 38.3 %collective-permute-start.31 = (bf16[1024,512]{1,0:T(8,128)(2,1)S(1)}, bf16[1024,512]{1,0:T(8,128)(2,1)S(1)}, u32[]{:S(2)}, u32[]{:S(2)}) collective-permute-start(bf16[1024,512]{1,0:T(8,128)(2,1)S(1)} %pad_maximum_fusion.16), channel_id=1, source_target_pairs={{0,16},{8,24},{16,0},{24,8},{1,17},{9,25},{17,1},{25,9},{2,18},{10... | collective-permute-start | bytes 3145736 | tf_op jit(solution)/shard_map/ppermute | solution.py:285
  403.7 51.0 %collective-permute-start.25 = (bf16[512,1024]{1,0:T(8,128)(2,1)S(1)}, bf16[512,1024]{1,0:T(8,128)(2,1)S(1)}, u32[]{:S(2)}, u32[]{:S(2)}) collective-permute-start(bf16[512,1024]{1,0:T(8,128)(2,1)S(1)} %pad_maximum_fusion.13), channel_id=1, source_target_pairs={{0,8},{8,0},{16,24},{24,16},{1,9},{9,1},{17,25},{25,17},{2,10},{10... | collective-permute-start | bytes 3145736 | tf_op jit(solution)/shard_map/ppermute | solution.py:285
  414.9 39.7 %collective-permute-start.27 = (bf16[512,1024]{1,0:T(8,128)(2,1)S(1)}, bf16[512,1024]{1,0:T(8,128)(2,1)S(1)}, u32[]{:S(2)}, u32[]{:S(2)}) collective-permute-start(bf16[512,1024]{1,0:T(8,128)(2,1)S(1)} %pad_maximum_fusion.14), channel_id=1, source_target_pairs={{0,16},{8,24},{16,0},{24,8},{1,17},{9,25},{17,1},{25,9},{2,18},{10... | collective-permute-start | bytes 3145736 | tf_op jit(solution)/shard_map/ppermute | solution.py:285
  (157 other events, 1209.8 us)
Sparse Core Ops, SparseCore 0:
  11.2 49.8 all-gather.12
  63.2 45.8 all-gather.10
  110.8 45.8 all-gather.6
  158.1 45.8 all-gather.8
  206.1 48.7 reduce-scatter.8
  261.6 48.2 reduce-scatter.10
  312.2 48.1 reduce-scatter.4
  362.7 48.0 reduce-scatter.6
